TPU v7x, 32 devices: a whole 2x2x4 slice. The times are simulated.
32 devices in a mesh: groups: 2 (over y), gx: 4 (over x, core), gy: 4 (over z).
Axes of the slice: x: 2, y: 2, z: 4, core: 2. Of those that a mesh axis runs over, the one named last changes fastest.
Arguments:
- activations: bfloat16 [128, 8192], P(('groups', 'gy'), 'gx'), parts along dimension 0, may hold values from -6 to 6
- gate_quant: bfloat16 [8192, 30720], P('gx', 'gy'), may hold values from -0.0625 to 0.0625
- gate_scale: float32 [64, 240], P('gx', 'gy'), may hold values from 0.3 to 3
- up_quant: bfloat16 [8192, 30720], P('gx', 'gy'), may hold values from -0.0625 to 0.0625
- up_scale: float32 [64, 240], P('gx', 'gy'), may hold values from 0.3 to 3
- down_quant: bfloat16 [30720, 8192], P('gy', 'gx'), may hold values from -0.03125 to 0.03125
- down_scale: float32 [240, 64], P('gy', 'gx'), may hold values from 0.3 to 3
Outputs:
- ffn_out: bfloat16 [128, 8192], P(('groups', 'gy'), 'gx'), parts along dimension 0
There are 2 independent parts, one for each index of `groups`. A program takes and returns all parts, laid end to end along the dimension named above; an argument that names none is the same for every part. Nothing has to cross between parts.
All inputs are finite; a program needn't handle non-finite values.
Results may differ from a plain program's by a relative error of at most 0.0071.
Values may be sent and summed in bfloat16 or wider, within the bound.
No kernel may reach another device: no remote copies, remote signals or barrier semaphores. Data moves between devices by JAX's collectives and lax.ppermute only.
A program may use at most 256 MiB of HBM per device.

v0:
```python
import jax
import jax.numpy as jnp
from jax import lax
from jax.sharding import PartitionSpec as P

BLOCK = 128


def dequantize(quant, scales):
    rows_count = quant.shape[0]
    columns = quant.shape[1]
    spread = jnp.repeat(scales, BLOCK, axis=1)
    blocked = quant.reshape(rows_count // BLOCK, BLOCK, columns)
    scaled = blocked.astype(jnp.float32) * spread[:, None, :]
    return scaled.astype(jnp.bfloat16).reshape(rows_count, columns)


def swiglu(summed):
    middle = summed.shape[1] // 2
    return (jax.nn.silu(summed[:, :middle]) * summed[:, middle:]).astype(jnp.bfloat16)


def body(activations, gate_quant, gate_scale, up_quant, up_scale, down_quant, down_scale):
    gate_weight = dequantize(gate_quant, gate_scale)
    up_weight = dequantize(up_quant, up_scale)
    gathered_rows = lax.all_gather(activations, "gy", axis=0, tiled=True)
    gate = jnp.dot(gathered_rows, gate_weight, preferred_element_type=jnp.float32)
    up_values = jnp.dot(gathered_rows, up_weight, preferred_element_type=jnp.float32)
    partials = jnp.concatenate([gate, up_values], axis=1)
    shares = lax.psum_scatter(partials, "gx", scatter_dimension=0, tiled=True)
    hidden = lax.all_gather(swiglu(shares), "gx", axis=0, tiled=True)
    down_weight = dequantize(down_quant, down_scale)
    summed = lax.psum_scatter(
        jnp.dot(hidden, down_weight, preferred_element_type=jnp.float32),
        "gy",
        scatter_dimension=0,
        tiled=True,
    )
    return summed.astype(jnp.bfloat16)


def solution(mesh):
    placed = (
        P(("groups", "gy"), "gx"),
        P("gx", "gy"),
        P("gx", "gy"),
        P("gx", "gy"),
        P("gx", "gy"),
        P("gy", "gx"),
        P("gy", "gx"),
    )
    return jax.shard_map(
        body, mesh=mesh, in_specs=placed, out_specs=P(("groups", "gy"), "gx"), check_vma=False
    )
```

profile of v0, /device:TPU:0, one launch (start us, length us, event | category | flops | bytes accessed | tf_op | source)
XLA Modules:
  0.0 195.1 jit_solution(9300943705821022839)
XLA Ops:
  6.5 0.0 reduce-scatter.3.cloned.1.call-start
  6.5 15.8 %all_gather.6 = bf16[64,2048]{1,0:T(8,128)(2,1)S(1)} all-gather(bf16[16,2048]{1,0:T(8,128)(2,1)} %param.7), channel_id=1, replica_groups=mesh['groups'=2,'gx'=4,'gy'=4] {'gy'}, dimensions={0}, use_global_device_ids=true | all-gather | bytes 327680 | tf_op jit(solution)/shard_map/all_gather | solution.py:26
  22.4 0.9 broadcast_in_dim.10
  23.3 0.3 copy.15
  23.6 0.9 broadcast_in_dim.9
  24.5 0.3 copy.16
  24.7 21.6 %fusion.1 = bf16[2048,7680]{1,0:T(8,128)(2,1)} fusion(bf16[2048,7680]{1,0:T(8,128)(2,1)} %param.10, f32[16,7680]{1,0:T(8,128)S(1)} %bitcast.38), kind=kLoop, calls=%fused_computation.3 | loop fusion | flops 47185920 | bytes 63406080 | tf_op jit(solution)/shard_map/convert_element_type | solution.py:15
  46.4 12.8 %convolution_bitcast_fusion = f32[64,7680]{1,0:T(8,128)S(1)} fusion(bf16[64,2048]{1,0:T(8,128)(2,1)S(1)} %all_gather.6, bf16[2048,7680]{1,0:T(8,128)(2,1)} %fusion.1), kind=kOutput, calls=%fused_computation.6 | convolution fusion | flops 2013265920 | bytes 33685504 | tf_op jit(solution)/shard_map/dot_general | solution.py:28
  59.1 21.6 %fusion.2 = bf16[2048,7680]{1,0:T(8,128)(2,1)} fusion(bf16[2048,7680]{1,0:T(8,128)(2,1)} %param.8, f32[16,7680]{1,0:T(8,128)S(1)} %bitcast.37), kind=kLoop, calls=%fused_computation.5 | loop fusion | flops 47185920 | bytes 63406080 | tf_op jit(solution)/shard_map/convert_element_type | solution.py:15
  80.7 0.0 copy-start
  80.7 12.8 %convolution_bitcast_fusion.1 = f32[64,7680]{1,0:T(8,128)S(1)} fusion(bf16[64,2048]{1,0:T(8,128)(2,1)S(1)} %all_gather.6, bf16[2048,7680]{1,0:T(8,128)(2,1)} %fusion.2), kind=kOutput, calls=%fused_computation.7 | convolution fusion | flops 2013265920 | bytes 33685504 | tf_op jit(solution)/shard_map/dot_general | solution.py:27
  93.5 2.1 %pad_maximum_fusion = f32[64,15360]{1,0:T(8,128)} fusion(f32[64,7680]{1,0:T(8,128)S(1)} %convolution_bitcast_fusion, f32[64,7680]{1,0:T(8,128)S(1)} %convolution_bitcast_fusion.1), kind=kLoop, calls=%fused_computation.8 | loop fusion | flops 983040 | bytes 7864320 | tf_op jit(solution)/shard_map/concatenate | solution.py:29
  95.7 0.0 reduce-scatter.3.cloned.1.call-update
  95.7 0.0 reduce-scatter.5.cloned.1.call-start
  95.7 0.0 copy-done
  95.7 0.1 copy.9
  95.8 0.2 broadcast_in_dim.11
  96.1 0.2 copy.12
  96.2 23.0 %fusion = bf16[7680,2048]{1,0:T(8,128)(2,1)} fusion(bf16[7680,2048]{1,0:T(8,128)(2,1)} %param.12, f32[60,2048]{1,0:T(8,128)S(1)} %bitcast.33), kind=kLoop, calls=%fused_computation.1 | loop fusion | flops 47185920 | bytes 63406080 | tf_op jit(solution)/shard_map/convert_element_type | solution.py:15
  119.2 21.1 %reduce-scatter.3.cloned.1.call-done = f32[16,15360]{1,0:T(8,128)} async-done(((f32[64,15360]{1,0:T(8,128)}), f32[16,15360]{1,0:T(8,128)}) %reduce-scatter.3.cloned.1.call-update) | async-done | bytes 983056 | tf_op jit(solution)/shard_map/reduce_scatter | solution.py:30
  140.3 1.3 fusion.3
  141.6 9.3 %all_gather.7 = bf16[64,7680]{1,0:T(8,128)(2,1)S(1)} all-gather(bf16[16,7680]{1,0:T(8,128)(2,1)S(1)} %fusion.3), channel_id=1, replica_groups=mesh['groups'=2,'gx'=4,'gy'=4] {'gx'}, dimensions={0}, use_global_device_ids=true | all-gather | bytes 1228800 | tf_op jit(solution)/shard_map/all_gather | solution.py:31
  150.9 13.6 %fusion.4 = f32[64,2048]{1,0:T(8,128)} fusion(bf16[64,7680]{1,0:T(8,128)(2,1)S(1)} %all_gather.7, bf16[7680,2048]{1,0:T(8,128)(2,1)} %fusion), kind=kOutput, calls=%fused_computation.13 | convolution fusion | flops 2013265920 | bytes 32964608 | tf_op jit(solution)/shard_map/dot_general | solution.py:34
  164.5 0.0 reduce-scatter.5.cloned.1.call-update
  164.5 22.2 %reduce-scatter.5.cloned.1.call-done = f32[16,2048]{1,0:T(8,128)} async-done(((f32[64,2048]{1,0:T(8,128)}), f32[16,2048]{1,0:T(8,128)}) %reduce-scatter.5.cloned.1.call-update) | async-done | bytes 131088 | tf_op jit(solution)/shard_map/reduce_scatter | solution.py:33
  186.7 1.5 convert_element_type.37
  (1 shorter events, 0.0 us)
Async XLA Ops:
  6.5 133.7 %reduce-scatter.3.cloned.1.call-start = ((), (), s32[]{:S(2)}) async-start(), calls=%async_computation.2 | async-start | bytes 4915200 | tf_op jit(solution)/shard_map/reduce_scatter | solution.py:30
  80.7 15.0 %copy-start = (f32[60,16]{0,1:T(8,128)S(1)}, f32[60,16]{0,1:T(8,128)}, u32[]{:S(2)}) copy-start(f32[60,16]{0,1:T(8,128)} %param.13) | copy-start | bytes 11524
  95.7 91.0 %reduce-scatter.5.cloned.1.call-start = ((), (), s32[]{:S(2)}) async-start(), calls=%async_computation.3 | async-start | bytes 655360 | tf_op jit(solution)/shard_map/reduce_scatter | solution.py:33
Sparse Core Ops, SparseCore 0:
  95.8 44.4 reduce-scatter.2
  164.6 22.0 reduce-scatter.4
where the time goes:
time: 195 us
  other arithmetic  71.2 us (37%)
  waiting for transfers between devices  43.3 us (22%)
  matrix products  39.1 us (20%)
  blocking collectives  25.1 us (13%)
  between operations  13.5 us (7%)
  local copies, waits for them, and re-layouts  2.83 us (1%)
    convert_element_type x3, other arithmetic, dequantize(): return scaled.astype(jnp.bfloat16).reshape(rows_count, columns)  66.2 us
    reduce_scatter x1, waiting for transfers between devices, body(): lax.psum_scatter(jnp.dot(hidden, down_weight, preferred_element_type=jnp....  22.2 us
    reduce_scatter x1, waiting for transfers between devices, body(): shares = lax.psum_scatter(partials, 'gx', scatter_dimension=0, tiled=True)  21.1 us
    all_gather x1, blocking collectives, body(): gathered_rows = lax.all_gather(activations, 'gy', axis=0, tiled=True)  15.8 us
    dot_general x1, matrix products, body(): jnp.dot(hidden, down_weight, preferred_element_type=jnp.float32)  13.6 us
    dot_general x1, matrix products, body(): jnp.dot(gathered_rows, gate_weight, preferred_element_type=jnp.float32)  12.8 us
    dot_general x1, matrix products, body(): jnp.dot(gathered_rows, up_weight, preferred_element_type=jnp.float32)  12.8 us
    all_gather x1, blocking collectives, body(): hidden = lax.all_gather(swiglu(shares), 'gx', axis=0, tiled=True)  9.29 us
  transfers between devices with their start and end apart: 2, of which 2 were waited for; matrix products, arithmetic and copies ran while one was open for 12% of the time, Pallas kernels for 0%

commit v1 on v0

v1 whole, which is shorter than its diff:
```python
import functools

import jax
import jax.numpy as jnp
from jax import lax
from jax.experimental import pallas as pl
from jax.experimental.pallas import tpu as pltpu
from jax.sharding import PartitionSpec as P

BLOCK = 128
SPLIT = (0.4, 0.4, 0.2)
VMEM_LIMIT = 40 * 2**20


def bits_of(count):
    return count.bit_length() - 1


def reverse_bits(value, count):
    out = 0
    for _ in range(bits_of(count)):
        out, value = out * 2 + value % 2, value // 2
    return out


def swap(value, axis, size, step):
    return lax.ppermute(value, axis, [(i, i ^ step) for i in range(size)])


def chunk_sizes(blocks):
    sizes, done = [], 0
    for at in range(len(SPLIT)):
        upto = blocks if at == len(SPLIT) - 1 else round(blocks * sum(SPLIT[: at + 1]))
        sizes.append(upto - done)
        done = upto
    return [size for size in sizes if size > 0]


def load_rows(gx, refs, xs, wide):
    me = lax.axis_index("gx")
    per = refs[0].shape[0]
    sub = per * len(refs) // gx
    target = xs if sub % 16 == 0 else wide
    for slot in range(gx):
        for block in range(gx):

            @pl.when(me == block ^ reverse_bits(slot, gx))
            def _():
                first = block * sub
                if sub % per == 0:
                    for i in range(sub // per):
                        target[slot * sub + i * per : slot * sub + (i + 1) * per, :] = refs[first // per + i][...].astype(target.dtype)
                else:
                    value = refs[first // per][...].astype(target.dtype)
                    target[slot * sub : (slot + 1) * sub, :] = value[first % per : first % per + sub, :]

    if target is wide:
        xs[...] = wide[...].astype(xs.dtype)


def add_blocks(acc, xs, w, scale, row0, col0, depth):
    width = w.shape[1]

    def one(k, first):
        rows = pl.ds(pl.multiple_of(k * BLOCK, BLOCK), BLOCK)
        part = jnp.dot(xs[:, rows], w[rows, :], preferred_element_type=jnp.float32)
        pieces = [
            part[:, c * BLOCK : (c + 1) * BLOCK] * scale[row0 + k, col0 + c]
            for c in range(width // BLOCK)
        ]
        part = jnp.concatenate(pieces, axis=1)
        acc[...] = acc[...] + part

    for i in range(depth[1]):
        one(depth[0] + i, False)


def piece_blocks(blocks):
    return 2 if blocks % 2 == 0 else 1


def gate_up_kernel(gx, gy, block0, *refs):
    rows = refs[:gy]
    gate_q, up_q, gate_s, up_s, keep, send, xs, wide, gate_w, up_w, gate, up, sems = refs[gy:]
    blocks = gate_w.shape[0] // BLOCK
    width = gate_w.shape[1]
    step = piece_blocks(blocks)
    deep = step * BLOCK

    def copies(p):
        at = pl.ds(pl.multiple_of(p * deep, deep), deep)
        cols = pl.ds(block0 * BLOCK, width)
        return (
            pltpu.make_async_copy(gate_q.at[at, cols], gate_w.at[at, :], sems.at[0, p]),
            pltpu.make_async_copy(up_q.at[at, cols], up_w.at[at, :], sems.at[1, p]),
        )

    for p in range(blocks // step):
        for copy in copies(p):
            copy.start()
    load_rows(gx, rows, xs, wide)
    gate[...] = jnp.zeros_like(gate)
    up[...] = jnp.zeros_like(up)

    def body(p, carry):
        first, second = copies(p)
        first.wait()
        add_blocks(gate, xs, gate_w, gate_s, 0, block0, (p * step, step))
        second.wait()
        add_blocks(up, xs, up_w, up_s, 0, block0, (p * step, step))
        return carry

    lax.fori_loop(0, blocks // step, body, 0)
    half = keep.shape[0]
    keep[:, :width] = gate[:half, :]
    keep[:, width:] = up[:half, :]
    send[:, :width] = gate[half:, :].astype(send.dtype)
    send[:, width:] = up[half:, :].astype(send.dtype)


def gate_up(gx, gy, block0, count, rows, gate_q, up_q, gate_s, up_s):
    depth = gate_q.shape[0]
    total = rows[0].shape[0] * gy
    width = count * BLOCK
    pieces = depth // BLOCK // piece_blocks(depth // BLOCK)
    whole = pl.BlockSpec(memory_space=pltpu.VMEM)
    return pl.pallas_call(
        functools.partial(gate_up_kernel, gx, gy, block0),
        out_shape=(
            jax.ShapeDtypeStruct((total // 2, 2 * width), jnp.float32),
            jax.ShapeDtypeStruct((total // 2, 2 * width), jnp.bfloat16),
        ),
        in_specs=[whole] * gy
        + [pl.BlockSpec(memory_space=pl.ANY)] * 2
        + [pl.BlockSpec(memory_space=pltpu.SMEM)] * 2,
        out_specs=(whole, whole),
        scratch_shapes=[
            pltpu.VMEM((total, depth), jnp.bfloat16),
            pltpu.VMEM((total, depth), jnp.float32),
            pltpu.VMEM((depth, width), jnp.bfloat16),
            pltpu.VMEM((depth, width), jnp.bfloat16),
            pltpu.VMEM((total, width), jnp.float32),
            pltpu.VMEM((total, width), jnp.float32),
            pltpu.SemaphoreType.DMA((2, pieces)),
        ],
        cost_estimate=pl.CostEstimate(
            flops=4 * total * depth * width, bytes_accessed=4 * depth * width, transcendentals=0
        ),
        compiler_params=pltpu.CompilerParams(vmem_limit_bytes=VMEM_LIMIT),
    )(*rows, gate_q, up_q, gate_s, up_s)


def down_kernel(gx, gy, block0, parts, last, has_prior, *refs):
    hidden = refs[:parts]
    refs = refs[parts:]
    prior = None
    if has_prior:
        prior, refs = refs[0], refs[1:]
    down_q, down_s = refs[:2]
    outs = refs[2:-4] if last else refs[2:3]
    xs, w, acc, sems = refs[-4:]
    blocks = w.shape[0] // BLOCK
    step = piece_blocks(blocks)
    deep = step * BLOCK

    def copy(p):
        at = pl.multiple_of(p * deep, deep)
        return pltpu.make_async_copy(
            down_q.at[pl.ds(block0 * BLOCK + at, deep), :], w.at[pl.ds(at, deep), :], sems.at[p]
        )

    for p in range(blocks // step):
        copy(p).start()
    at = 0
    for ref in hidden:
        xs[at : at + ref.shape[0], :] = ref[...].astype(xs.dtype)
        at += ref.shape[0]
    if prior is None:
        acc[...] = jnp.zeros_like(acc)
    else:
        acc[...] = prior[...]

    def body(p, carry):
        copy(p).wait()
        add_blocks(acc, xs, w, down_s, block0, 0, (p * step, step))
        return carry

    lax.fori_loop(0, blocks // step, body, 0)
    if not last:
        outs[0][...] = acc[...]
        return
    me = lax.axis_index("gx")
    per = outs[0].shape[0]
    sub = xs.shape[0] // gx
    for slot in range(gx):
        for block in range(gx):

            @pl.when(me == block ^ reverse_bits(slot, gx))
            def _():
                first = block * sub
                if sub % per == 0:
                    for i in range(sub // per):
                        out = outs[first // per + i]
                        out[...] = acc[slot * sub + i * per : slot * sub + (i + 1) * per, :].astype(out.dtype)
                else:
                    out = outs[first // per]
                    out[first % per : first % per + sub, :] = acc[slot * sub : (slot + 1) * sub, :].astype(out.dtype)


def down(gx, gy, block0, count, hidden, prior, down_q, down_s, last):
    total = sum(part.shape[0] for part in hidden)
    depth, width = count * BLOCK, down_q.shape[1]
    whole = pl.BlockSpec(memory_space=pltpu.VMEM)
    per = total // gy
    if last:
        sent = jnp.bfloat16 if per // 16 * 16 == per and total // gx % 16 == 0 else jnp.float32
        out_shape = [jax.ShapeDtypeStruct((per, width), jnp.float32 if r == 0 else sent) for r in range(gy)]
    else:
        out_shape = [jax.ShapeDtypeStruct((total, width), jnp.float32)]
    before = [] if prior is None else [prior]
    return pl.pallas_call(
        functools.partial(down_kernel, gx, gy, block0, len(hidden), last, prior is not None),
        out_shape=out_shape,
        in_specs=[whole] * (len(hidden) + len(before))
        + [pl.BlockSpec(memory_space=pl.ANY), pl.BlockSpec(memory_space=pltpu.SMEM)],
        out_specs=[whole] * len(out_shape),
        scratch_shapes=[
            pltpu.VMEM((total, depth), jnp.bfloat16),
            pltpu.VMEM((depth, width), jnp.bfloat16),
            pltpu.VMEM((total, width), jnp.float32),
            pltpu.SemaphoreType.DMA((count // piece_blocks(count),)),
        ],
        cost_estimate=pl.CostEstimate(
            flops=2 * total * depth * width, bytes_accessed=2 * depth * width, transcendentals=0
        ),
        compiler_params=pltpu.CompilerParams(vmem_limit_bytes=VMEM_LIMIT),
    )(*hidden, *before, down_q, down_s)


def reduce_and_activate(gx, keep, send):
    for step in range(bits_of(gx)):
        got = swap(send, "gx", gx, 1 << step)
        total = keep + got.astype(jnp.float32)
        if step < bits_of(gx) - 1:
            half = total.shape[0] // 2
            keep, send = total[:half], total[half:].astype(jnp.bfloat16)
    middle = total.shape[1] // 2
    return (jax.nn.silu(total[:, :middle]) * total[:, middle:]).astype(jnp.bfloat16)


def spread(gx, own):
    held = [own]
    for step in reversed(range(bits_of(gx))):
        held = held + [swap(block, "gx", gx, 1 << step) for block in held]
    return held


def body(gx, gy, activations, gate_q, gate_s, up_q, up_s, down_q, down_s):
    rows = [activations] + [swap(activations, "gy", gy, r) for r in range(1, gy)]
    counts = chunk_sizes(gate_q.shape[1] // BLOCK)
    starts = [sum(counts[:i]) for i in range(len(counts))]
    hidden = []
    for block0, count in zip(starts, counts):
        keep, send = gate_up(gx, gy, block0, count, rows, gate_q, up_q, gate_s, up_s)
        hidden.append(spread(gx, reduce_and_activate(gx, keep, send)))
    prior = None
    for i, (block0, count) in enumerate(zip(starts, counts)):
        last = i == len(counts) - 1
        outs = down(gx, gy, block0, count, hidden[i], prior, down_q, down_s, last)
        prior = outs[0]
    total = outs[0]
    for r in range(1, gy):
        total = total + swap(outs[r], "gy", gy, r).astype(jnp.float32)
    return total.astype(jnp.bfloat16)


def solution(mesh):
    placed = (
        P(("groups", "gy"), "gx"),
        P("gx", "gy"),
        P("gx", "gy"),
        P("gx", "gy"),
        P("gx", "gy"),
        P("gy", "gx"),
        P("gy", "gx"),
    )
    return jax.shard_map(
        functools.partial(body, mesh.shape["gx"], mesh.shape["gy"]),
        mesh=mesh,
        in_specs=placed,
        out_specs=P(("groups", "gy"), "gx"),
        check_vma=False,
    )
```

time: 195 us -> 88.8 us (0.46)
  other arithmetic: 71.2 us -> 1.1 us
  Pallas kernels: 0 us -> 42.4 us
  matrix products: 39.1 us -> 0 us
  blocking collectives: 25.1 us -> 0 us
  waiting for transfers between devices: 43.3 us -> 25 us
  starting transfers between devices: 0.04 us -> 17.4 us
  between operations: 13.5 us -> 0.2 us
    convert_element_type x5 -> x4, other arithmetic: 69 us -> 0.83 us  [the longest x1 0.66 us: body(): return total.astype(jnp.bfloat16)]
    reduce_scatter x2 -> x0, waiting for transfers between devices: 43.3 us -> none  [the longest x1 22.2 us: body(): lax.psum_scatter(jnp.dot(hidden, down_weight, preferred_element_type=jnp....]
    pallas_call x0 -> x6, Pallas kernels: none -> 42.4 us  [the longest x3 25.7 us: gate_up(): pl.pallas_call(functools.partial(gate_up_kernel, gx, gy, block0), out_sha...]
    dot_general x3 -> x0, matrix products: 39.1 us -> none  [the longest x1 13.6 us: body(): jnp.dot(hidden, down_weight, preferred_element_type=jnp.float32)]
    all_gather x2 -> x0, blocking collectives: 25.1 us -> none  [the longest x1 15.8 us: body(): gathered_rows = lax.all_gather(activations, 'gy', axis=0, tiled=True)]
    ppermute x0 -> x21, waiting for transfers between devices: none -> 25 us  [swap(): return lax.ppermute(value, axis, [(i, i ^ step) for i in range(size)])]
    ppermute x0 -> x21, starting transfers between devices: none -> 17.4 us  [swap(): return lax.ppermute(value, axis, [(i, i ^ step) for i in range(size)])]
    concatenate x1 -> x0, other arithmetic: 2.13 us -> none  [body(): partials = jnp.concatenate([gate, up_values], axis=1)]
  transfers between devices with their start and end apart: 2 -> 21, of which waited for: 2 -> 10; matrix products, arithmetic and copies ran while one was open for 12% -> 1% of each run, Pallas kernels for 0% -> 36%
where the time goes in v1:
time: 88.8 us; the launch traced here: 88.5 us
  Pallas kernels  42.4 us (48%)
  waiting for transfers between devices  25 us (28%)
  starting transfers between devices  17.4 us (20%)
  local copies, waits for them, and re-layouts  2.39 us (3%)
  other arithmetic  1.1 us (1%)
    pallas_call x3, Pallas kernels, gate_up(): pl.pallas_call(functools.partial(gate_up_kernel, gx, gy, block0), out_sha...  25.7 us
    ppermute x21, waiting for transfers between devices, swap(): return lax.ppermute(value, axis, [(i, i ^ step) for i in range(size)])  25 us
    ppermute x21, starting transfers between devices, swap(): return lax.ppermute(value, axis, [(i, i ^ step) for i in range(size)])  17.4 us
    pallas_call x3, Pallas kernels, down(): pl.pallas_call(functools.partial(down_kernel, gx, gy, block0, len(hidden)...  16.7 us
    unnamed x9, local copies, waits for them, and re-layouts  2.33 us
  transfers between devices with their start and end apart: 21, of which 10 were waited for; matrix products, arithmetic and copies ran while one was open for 1% of the time, Pallas kernels for 36%

profile of v1, /device:TPU:0, one launch (start us, length us, event | category | flops | bytes accessed | tf_op | source)
XLA Modules:
  0.0 88.5 jit_solution(5152592585943658454)
XLA Ops:
  0.0 3.0 %collective-permute-start = (bf16[16,2048]{1,0:T(8,128)(2,1)}, bf16[16,2048]{1,0:T(8,128)(2,1)S(1)}, u32[]{:S(2)}, u32[]{:S(2)}) collective-permute-start(bf16[16,2048]{1,0:T(8,128)(2,1)} %refs_0_.5), channel_id=1, source_target_pairs={{0,1},{1,0},{2,3},{3,2},{4,5},{5,4},{6,7},{7,6},{8,9},{9,8},{10,11... | collective-permute-start | bytes 196616 | tf_op jit(solution)/shard_map/ppermute | solution.py:27
  3.0 2.6 %collective-permute-start.1 = (bf16[16,2048]{1,0:T(8,128)(2,1)}, bf16[16,2048]{1,0:T(8,128)(2,1)S(1)}, u32[]{:S(2)}, u32[]{:S(2)}) collective-permute-start(bf16[16,2048]{1,0:T(8,128)(2,1)} %refs_0_.5), channel_id=1, source_target_pairs={{0,2},{1,3},{2,0},{3,1},{4,6},{5,7},{6,4},{7,5},{8,10},{9,11},{10,... | collective-permute-start | bytes 196616 | tf_op jit(solution)/shard_map/ppermute | solution.py:27
  5.6 0.0 collective-permute-start.2
  5.6 0.0 collective-permute-done.refs_1_
  5.6 4.9 %collective-permute-done.1.refs_2_ = bf16[16,2048]{1,0:T(8,128)(2,1)S(1)} collective-permute-done((bf16[16,2048]{1,0:T(8,128)(2,1)}, bf16[16,2048]{1,0:T(8,128)(2,1)S(1)}, u32[]{:S(2)}, u32[]{:S(2)}) %collective-permute-start.1) | collective-permute-done | bytes 65568 | tf_op jit(solution)/shard_map/ppermute | solution.py:27
  10.5 1.4 %collective-permute-done.2.refs_3_ = bf16[16,2048]{1,0:T(8,128)(2,1)S(1)} collective-permute-done((bf16[16,2048]{1,0:T(8,128)(2,1)}, bf16[16,2048]{1,0:T(8,128)(2,1)S(1)}, u32[]{:S(2)}, u32[]{:S(2)}) %collective-permute-start.2) | collective-permute-done | bytes 65568 | tf_op jit(solution)/shard_map/ppermute | solution.py:27
  11.9 0.0 copy-start
  11.9 0.8 copy-done
  12.8 0.0 copy-start.1
  12.8 0.7 copy-done.1
  13.5 0.0 copy-start.2
  13.5 0.7 copy-done.2
  14.2 6.4 %shard_map.73 = (f32[32,3072]{1,0:T(8,128)S(1)}, bf16[32,3072]{1,0:T(8,128)(2,1)S(1)}) custom-call(bf16[16,2048]{1,0:T(8,128)(2,1)S(1)} %copy-done, bf16[16,2048]{1,0:T(8,128)(2,1)S(1)} %collective-permute-done.refs_1_, bf16[16,2048]{1,0:T(8,128)(2,1)S(1)} %collective-permute-done.1.refs_2_, bf16[16,2048]{1,0:T(8,128)(2,1)S(1)} %collective-permute-done.2.refs_3_, ...), custom_call_target="tpu_custom_call" | custom-call | flops 805306368 | bytes 12582912 | tf_op jit(solution)/shard_map/pallas_call | solution.py:127
  20.6 0.1 collective-permute-start.3
  20.6 9.6 %shard_map.74 = (f32[32,6144]{1,0:T(8,128)S(1)}, bf16[32,6144]{1,0:T(8,128)(2,1)S(1)}) custom-call(bf16[16,2048]{1,0:T(8,128)(2,1)S(1)} %copy-done, bf16[16,2048]{1,0:T(8,128)(2,1)S(1)} %collective-permute-done.refs_1_, bf16[16,2048]{1,0:T(8,128)(2,1)S(1)} %collective-permute-done.1.refs_2_, bf16[16,2048]{1,0:T(8,128)(2,1)S(1)} %collective-permute-done.2.refs_3_, ...), custom_call_target="tpu_custom_call" | custom-call | flops 1610612736 | bytes 25165824 | tf_op jit(solution)/shard_map/pallas_call | solution.py:127
  30.2 0.6 collective-permute-start.8
  30.8 0.0 collective-permute-done.3
  30.9 0.0 copy-start.3
  30.9 1.6 %collective-permute-start.4 = (bf16[16,3072]{1,0:T(8,128)(2,1)S(1)}, bf16[16,3072]{1,0:T(8,128)(2,1)S(1)}, u32[]{:S(2)}, u32[]{:S(2)}) collective-permute-start(bf16[16,3072]{1,0:T(8,128)(2,1)S(1)} %slice.83), channel_id=1, source_target_pairs={{0,8},{4,12},{8,0},{12,4},{1,9},{5,13},{9,1},{13,5},{2,10},{6,14},... | collective-permute-start | bytes 294920 | tf_op jit(solution)/shard_map/ppermute | solution.py:27
  32.4 9.7 %shard_map.75 = (f32[32,6144]{1,0:T(8,128)S(1)}, bf16[32,6144]{1,0:T(8,128)(2,1)S(1)}) custom-call(bf16[16,2048]{1,0:T(8,128)(2,1)S(1)} %copy-done, bf16[16,2048]{1,0:T(8,128)(2,1)S(1)} %collective-permute-done.refs_1_, bf16[16,2048]{1,0:T(8,128)(2,1)S(1)} %collective-permute-done.1.refs_2_, bf16[16,2048]{1,0:T(8,128)(2,1)S(1)} %collective-permute-done.2.refs_3_, ...), custom_call_target="tpu_custom_call" | custom-call | flops 1610612736 | bytes 25165824 | tf_op jit(solution)/shard_map/pallas_call | solution.py:127
  42.2 0.1 collective-permute-start.13
  42.3 0.0 collective-permute-done.4
  42.3 1.7 %collective-permute-done.13 = bf16[32,6144]{1,0:T(8,128)(2,1)S(1)} collective-permute-done((bf16[32,6144]{1,0:T(8,128)(2,1)S(1)}, bf16[32,6144]{1,0:T(8,128)(2,1)S(1)}, u32[]{:S(2)}, u32[]{:S(2)}) %collective-permute-start.13) | collective-permute-done | bytes 393248 | tf_op jit(solution)/shard_map/ppermute | solution.py:27
  44.0 0.1 convert_add_fusion
  44.1 0.6 collective-permute-start.14
  44.7 0.0 collective-permute-done.8
  44.7 0.1 convert_add_fusion.1
  44.8 1.6 %collective-permute-start.9 = (bf16[16,6144]{1,0:T(8,128)(2,1)S(1)}, bf16[16,6144]{1,0:T(8,128)(2,1)S(1)}, u32[]{:S(2)}, u32[]{:S(2)}) collective-permute-start(bf16[16,6144]{1,0:T(8,128)(2,1)S(1)} %slice.82), channel_id=1, source_target_pairs={{0,8},{4,12},{8,0},{12,4},{1,9},{5,13},{9,1},{13,5},{2,10},{6,14},... | collective-permute-start | bytes 589832 | tf_op jit(solution)/shard_map/ppermute | solution.py:27
  46.3 5.5 %collective-permute-done.14 = bf16[16,6144]{1,0:T(8,128)(2,1)S(1)} collective-permute-done((bf16[16,6144]{1,0:T(8,128)(2,1)S(1)}, bf16[16,6144]{1,0:T(8,128)(2,1)S(1)}, u32[]{:S(2)}, u32[]{:S(2)}) %collective-permute-start.14) | collective-permute-done | bytes 196640 | tf_op jit(solution)/shard_map/ppermute | solution.py:27
  51.9 0.1 fusion.refs_0_
  52.0 0.6 collective-permute-start.15
  52.6 0.0 collective-permute-start.16
  52.6 3.5 %collective-permute-done.9 = bf16[16,6144]{1,0:T(8,128)(2,1)S(1)} collective-permute-done((bf16[16,6144]{1,0:T(8,128)(2,1)S(1)}, bf16[16,6144]{1,0:T(8,128)(2,1)S(1)}, u32[]{:S(2)}, u32[]{:S(2)}) %collective-permute-start.9) | collective-permute-done | bytes 196640 | tf_op jit(solution)/shard_map/ppermute | solution.py:27
  56.2 0.1 fusion.1.refs_0_
  56.2 0.6 collective-permute-start.10
  56.8 0.6 collective-permute-done.15.refs_1_
  57.4 0.0 collective-permute-start.17
  57.5 1.0 %collective-permute-start.5 = (bf16[16,1536]{1,0:T(8,128)(2,1)S(1)}, bf16[16,1536]{1,0:T(8,128)(2,1)S(1)}, u32[]{:S(2)}, u32[]{:S(2)}) collective-permute-start(bf16[16,1536]{1,0:T(8,128)(2,1)S(1)} %fusion.2.refs_0_), channel_id=1, source_target_pairs={{0,8},{4,12},{8,0},{12,4},{1,9},{5,13},{9,1},{13,5},{2,10},{6,14},... | collective-permute-start | bytes 147464 | tf_op jit(solution)/shard_map/ppermute | solution.py:27
  58.4 0.2 collective-permute-start.11
  58.7 2.6 %collective-permute-done.10.refs_1_ = bf16[16,3072]{1,0:T(8,128)(2,1)S(1)} collective-permute-done((bf16[16,3072]{1,0:T(8,128)(2,1)S(1)}, bf16[16,3072]{1,0:T(8,128)(2,1)S(1)}, u32[]{:S(2)}, u32[]{:S(2)}) %collective-permute-start.10) | collective-permute-done | bytes 98336 | tf_op jit(solution)/shard_map/ppermute | solution.py:27
  61.2 0.0 collective-permute-start.12
  61.2 0.0 copy-done.3
  61.2 0.1 copy.8.refs_5_.refs_6_
  61.3 0.6 collective-permute-done.5.refs_1_
  62.0 0.0 collective-permute-start.6
  62.0 0.0 collective-permute-done.16.refs_2_
  62.0 0.5 collective-permute-start.7
  62.5 0.0 collective-permute-done.17.refs_3_
  62.5 6.2 %shard_map.76.refs_4_ = f32[64,2048]{1,0:T(8,128)S(1)} custom-call(bf16[16,3072]{1,0:T(8,128)(2,1)S(1)} %fusion.refs_0_, bf16[16,3072]{1,0:T(8,128)(2,1)S(1)} %collective-permute-done.15.refs_1_, bf16[16,3072]{1,0:T(8,128)(2,1)S(1)} %collective-permute-done.16.refs_2_, bf16[16,3072]{1,0:T(8,128)(2,1)S(1)} %collective-permute-done.17.refs_3_, ...), custom_call_target="tpu_custom_call" | custom-call | flops 805306368 | bytes 12582912 | tf_op jit(solution)/shard_map/pallas_call | solution.py:221
  68.7 0.0 collective-permute-done.11.refs_2_
  68.7 0.0 collective-permute-done.12.refs_3_
  68.7 6.2 %shard_map.77.refs_4_ = f32[64,2048]{1,0:T(8,128)S(1)} custom-call(bf16[16,3072]{1,0:T(8,128)(2,1)S(1)} %fusion.1.refs_0_, bf16[16,3072]{1,0:T(8,128)(2,1)S(1)} %collective-permute-done.10.refs_1_, bf16[16,3072]{1,0:T(8,128)(2,1)S(1)} %collective-permute-done.11.refs_2_, bf16[16,3072]{1,0:T(8,128)(2,1)S(1)} %collective-permute-done.12.refs_3_, ...), custom_call_target="tpu_custom_call" | custom-call | flops 805306368 | bytes 12582912 | tf_op jit(solution)/shard_map/pallas_call | solution.py:221
  74.9 0.0 collective-permute-done.6.refs_2_
  74.9 0.0 collective-permute-done.7.refs_3_
  74.9 4.3 %shard_map.78 = (f32[16,2048]{1,0:T(8,128)S(1)}, bf16[16,2048]{1,0:T(8,128)(2,1)S(1)}, bf16[16,2048]{1,0:T(8,128)(2,1)S(1)}, bf16[16,2048]{1,0:T(8,128)(2,1)S(1)}) custom-call(bf16[16,1536]{1,0:T(8,128)(2,1)S(1)} %fusion.2.refs_0_, bf16[16,1536]{1,0:T(8,128)(2,1)S(1)} %collective-permute-done.5.refs_1_, bf16[16,1536]{1,0:T(8,128)(2,1)S(1)} %collective-permute-done.6.refs_2_, ...), custom_call_target="tpu_custom_call" | custom-call | flops 402653184 | bytes 6291456 | tf_op jit(solution)/shard_map/pallas_call | solution.py:221
  79.2 1.8 %collective-permute-start.20 = (bf16[16,2048]{1,0:T(8,128)(2,1)S(1)}, bf16[16,2048]{1,0:T(8,128)(2,1)S(1)}, u32[]{:S(2)}, u32[]{:S(2)}) collective-permute-start(bf16[16,2048]{1,0:T(8,128)(2,1)S(1)} %get-tuple-element.24), channel_id=1, source_target_pairs={{0,3},{1,2},{2,1},{3,0},{4,7},{5,6},{6,5},{7,4},{8,11},{9,10},{10,... | collective-permute-start | bytes 196616 | tf_op jit(solution)/shard_map/ppermute | solution.py:27
  81.0 0.0 collective-permute-start.19
  81.0 2.6 %collective-permute-start.18 = (bf16[16,2048]{1,0:T(8,128)(2,1)S(1)}, bf16[16,2048]{1,0:T(8,128)(2,1)S(1)}, u32[]{:S(2)}, u32[]{:S(2)}) collective-permute-start(bf16[16,2048]{1,0:T(8,128)(2,1)S(1)} %get-tuple-element.22), channel_id=1, source_target_pairs={{0,1},{1,0},{2,3},{3,2},{4,5},{5,4},{6,7},{7,6},{8,9},{9,8},{10,11... | collective-permute-start | bytes 196616 | tf_op jit(solution)/shard_map/ppermute | solution.py:27
  83.7 2.4 %collective-permute-done.20 = bf16[16,2048]{1,0:T(8,128)(2,1)S(1)} collective-permute-done((bf16[16,2048]{1,0:T(8,128)(2,1)S(1)}, bf16[16,2048]{1,0:T(8,128)(2,1)S(1)}, u32[]{:S(2)}, u32[]{:S(2)}) %collective-permute-start.20) | collective-permute-done | bytes 65568 | tf_op jit(solution)/shard_map/ppermute | solution.py:27
  86.1 1.8 %collective-permute-done.19 = bf16[16,2048]{1,0:T(8,128)(2,1)S(1)} collective-permute-done((bf16[16,2048]{1,0:T(8,128)(2,1)S(1)}, bf16[16,2048]{1,0:T(8,128)(2,1)S(1)}, u32[]{:S(2)}, u32[]{:S(2)}) %collective-permute-start.19) | collective-permute-done | bytes 65568 | tf_op jit(solution)/shard_map/ppermute | solution.py:27
  87.9 0.0 collective-permute-done.18
  87.9 0.7 add_convert_fusion
  (8 shorter events, 0.2 us)
Async XLA Ops:
  0.0 5.6 %collective-permute-start = (bf16[16,2048]{1,0:T(8,128)(2,1)}, bf16[16,2048]{1,0:T(8,128)(2,1)S(1)}, u32[]{:S(2)}, u32[]{:S(2)}) collective-permute-start(bf16[16,2048]{1,0:T(8,128)(2,1)} %refs_0_.5), channel_id=1, source_target_pairs={{0,1},{1,0},{2,3},{3,2},{4,5},{5,4},{6,7},{7,6},{8,9},{9,8},{10,11... | collective-permute-start | bytes 196616 | tf_op jit(solution)/shard_map/ppermute | solution.py:27
  3.0 7.5 %collective-permute-start.1 = (bf16[16,2048]{1,0:T(8,128)(2,1)}, bf16[16,2048]{1,0:T(8,128)(2,1)S(1)}, u32[]{:S(2)}, u32[]{:S(2)}) collective-permute-start(bf16[16,2048]{1,0:T(8,128)(2,1)} %refs_0_.5), channel_id=1, source_target_pairs={{0,2},{1,3},{2,0},{3,1},{4,6},{5,7},{6,4},{7,5},{8,10},{9,11},{10,... | collective-permute-start | bytes 196616 | tf_op jit(solution)/shard_map/ppermute | solution.py:27
  5.6 6.3 %collective-permute-start.2 = (bf16[16,2048]{1,0:T(8,128)(2,1)}, bf16[16,2048]{1,0:T(8,128)(2,1)S(1)}, u32[]{:S(2)}, u32[]{:S(2)}) collective-permute-start(bf16[16,2048]{1,0:T(8,128)(2,1)} %refs_0_.5), channel_id=1, source_target_pairs={{0,3},{1,2},{2,1},{3,0},{4,7},{5,6},{6,5},{7,4},{8,11},{9,10},{10,... | collective-permute-start | bytes 196616 | tf_op jit(solution)/shard_map/ppermute | solution.py:27
  11.9 0.8 copy-start
  12.8 0.7 copy-start.1
  13.5 0.7 copy-start.2
  20.6 10.3 %collective-permute-start.3 = (bf16[32,3072]{1,0:T(8,128)(2,1)S(1)}, bf16[32,3072]{1,0:T(8,128)(2,1)S(1)}, u32[]{:S(2)}, u32[]{:S(2)}) collective-permute-start(bf16[32,3072]{1,0:T(8,128)(2,1)S(1)} %get-tuple-element.16), channel_id=1, source_target_pairs={{0,4},{4,0},{8,12},{12,8},{1,5},{5,1},{9,13},{13,9},{2,6},{6,2},{1... | collective-permute-start | bytes 589832 | tf_op jit(solution)/shard_map/ppermute | solution.py:27
  30.2 14.4 %collective-permute-start.8 = (bf16[32,6144]{1,0:T(8,128)(2,1)S(1)}, bf16[32,6144]{1,0:T(8,128)(2,1)S(1)}, u32[]{:S(2)}, u32[]{:S(2)}) collective-permute-start(bf16[32,6144]{1,0:T(8,128)(2,1)S(1)} %get-tuple-element.18), channel_id=1, source_target_pairs={{0,4},{4,0},{8,12},{12,8},{1,5},{5,1},{9,13},{13,9},{2,6},{6,2},{1... | collective-permute-start | bytes 1179656 | tf_op jit(solution)/shard_map/ppermute | solution.py:27
  30.9 30.4 %copy-start.3 = (f32[60,16]{0,1:T(8,128)S(1)}, f32[60,16]{0,1:T(8,128)}, u32[]{:S(2)}) copy-start(f32[60,16]{0,1:T(8,128)} %param.13) | copy-start | bytes 11524
  30.9 11.4 %collective-permute-start.4 = (bf16[16,3072]{1,0:T(8,128)(2,1)S(1)}, bf16[16,3072]{1,0:T(8,128)(2,1)S(1)}, u32[]{:S(2)}, u32[]{:S(2)}) collective-permute-start(bf16[16,3072]{1,0:T(8,128)(2,1)S(1)} %slice.83), channel_id=1, source_target_pairs={{0,8},{4,12},{8,0},{12,4},{1,9},{5,13},{9,1},{13,5},{2,10},{6,14},... | collective-permute-start | bytes 294920 | tf_op jit(solution)/shard_map/ppermute | solution.py:27
  42.2 1.8 %collective-permute-start.13 = (bf16[32,6144]{1,0:T(8,128)(2,1)S(1)}, bf16[32,6144]{1,0:T(8,128)(2,1)S(1)}, u32[]{:S(2)}, u32[]{:S(2)}) collective-permute-start(bf16[32,6144]{1,0:T(8,128)(2,1)S(1)} %get-tuple-element.20), channel_id=1, source_target_pairs={{0,4},{4,0},{8,12},{12,8},{1,5},{5,1},{9,13},{13,9},{2,6},{6,2},{1... | collective-permute-start | bytes 1179656 | tf_op jit(solution)/shard_map/ppermute | solution.py:27
  44.1 7.8 %collective-permute-start.14 = (bf16[16,6144]{1,0:T(8,128)(2,1)S(1)}, bf16[16,6144]{1,0:T(8,128)(2,1)S(1)}, u32[]{:S(2)}, u32[]{:S(2)}) collective-permute-start(bf16[16,6144]{1,0:T(8,128)(2,1)S(1)} %slice.81), channel_id=1, source_target_pairs={{0,8},{4,12},{8,0},{12,4},{1,9},{5,13},{9,1},{13,5},{2,10},{6,14},... | collective-permute-start | bytes 589832 | tf_op jit(solution)/shard_map/ppermute | solution.py:27
  44.8 11.3 %collective-permute-start.9 = (bf16[16,6144]{1,0:T(8,128)(2,1)S(1)}, bf16[16,6144]{1,0:T(8,128)(2,1)S(1)}, u32[]{:S(2)}, u32[]{:S(2)}) collective-permute-start(bf16[16,6144]{1,0:T(8,128)(2,1)S(1)} %slice.82), channel_id=1, source_target_pairs={{0,8},{4,12},{8,0},{12,4},{1,9},{5,13},{9,1},{13,5},{2,10},{6,14},... | collective-permute-start | bytes 589832 | tf_op jit(solution)/shard_map/ppermute | solution.py:27
  52.0 5.4 %collective-permute-start.15 = (bf16[16,3072]{1,0:T(8,128)(2,1)S(1)}, bf16[16,3072]{1,0:T(8,128)(2,1)S(1)}, u32[]{:S(2)}, u32[]{:S(2)}) collective-permute-start(bf16[16,3072]{1,0:T(8,128)(2,1)S(1)} %fusion.refs_0_), channel_id=1, source_target_pairs={{0,8},{4,12},{8,0},{12,4},{1,9},{5,13},{9,1},{13,5},{2,10},{6,14},... | collective-permute-start | bytes 294920 | tf_op jit(solution)/shard_map/ppermute | solution.py:27
  52.6 9.4 %collective-permute-start.16 = (bf16[16,3072]{1,0:T(8,128)(2,1)S(1)}, bf16[16,3072]{1,0:T(8,128)(2,1)S(1)}, u32[]{:S(2)}, u32[]{:S(2)}) collective-permute-start(bf16[16,3072]{1,0:T(8,128)(2,1)S(1)} %fusion.refs_0_), channel_id=1, source_target_pairs={{0,4},{4,0},{8,12},{12,8},{1,5},{5,1},{9,13},{13,9},{2,6},{6,2},{1... | collective-permute-start | bytes 294920 | tf_op jit(solution)/shard_map/ppermute | solution.py:27
  56.2 5.0 %collective-permute-start.10 = (bf16[16,3072]{1,0:T(8,128)(2,1)S(1)}, bf16[16,3072]{1,0:T(8,128)(2,1)S(1)}, u32[]{:S(2)}, u32[]{:S(2)}) collective-permute-start(bf16[16,3072]{1,0:T(8,128)(2,1)S(1)} %fusion.1.refs_0_), channel_id=1, source_target_pairs={{0,8},{4,12},{8,0},{12,4},{1,9},{5,13},{9,1},{13,5},{2,10},{6,14},... | collective-permute-start | bytes 294920 | tf_op jit(solution)/shard_map/ppermute | solution.py:27
  57.4 5.1 %collective-permute-start.17 = (bf16[16,3072]{1,0:T(8,128)(2,1)S(1)}, bf16[16,3072]{1,0:T(8,128)(2,1)S(1)}, u32[]{:S(2)}, u32[]{:S(2)}) collective-permute-start(bf16[16,3072]{1,0:T(8,128)(2,1)S(1)} %collective-permute-done.15.refs_1_), channel_id=1, source_target_pairs={{0,4},{4,0},{8,12},{12,8},{1,5},{5,1},{9,13},{13,9},{2,6},{6,2},{1... | collective-permute-start | bytes 294920 | tf_op jit(solution)/shard_map/ppermute | solution.py:27
  57.5 4.5 %collective-permute-start.5 = (bf16[16,1536]{1,0:T(8,128)(2,1)S(1)}, bf16[16,1536]{1,0:T(8,128)(2,1)S(1)}, u32[]{:S(2)}, u32[]{:S(2)}) collective-permute-start(bf16[16,1536]{1,0:T(8,128)(2,1)S(1)} %fusion.2.refs_0_), channel_id=1, source_target_pairs={{0,8},{4,12},{8,0},{12,4},{1,9},{5,13},{9,1},{13,5},{2,10},{6,14},... | collective-permute-start | bytes 147464 | tf_op jit(solution)/shard_map/ppermute | solution.py:27
  58.4 10.2 %collective-permute-start.11 = (bf16[16,3072]{1,0:T(8,128)(2,1)S(1)}, bf16[16,3072]{1,0:T(8,128)(2,1)S(1)}, u32[]{:S(2)}, u32[]{:S(2)}) collective-permute-start(bf16[16,3072]{1,0:T(8,128)(2,1)S(1)} %fusion.1.refs_0_), channel_id=1, source_target_pairs={{0,4},{4,0},{8,12},{12,8},{1,5},{5,1},{9,13},{13,9},{2,6},{6,2},{1... | collective-permute-start | bytes 294920 | tf_op jit(solution)/shard_map/ppermute | solution.py:27
  61.2 7.4 %collective-permute-start.12 = (bf16[16,3072]{1,0:T(8,128)(2,1)S(1)}, bf16[16,3072]{1,0:T(8,128)(2,1)S(1)}, u32[]{:S(2)}, u32[]{:S(2)}) collective-permute-start(bf16[16,3072]{1,0:T(8,128)(2,1)S(1)} %collective-permute-done.10.refs_1_), channel_id=1, source_target_pairs={{0,4},{4,0},{8,12},{12,8},{1,5},{5,1},{9,13},{13,9},{2,6},{6,2},{1... | collective-permute-start | bytes 294920 | tf_op jit(solution)/shard_map/ppermute | solution.py:27
  62.0 12.9 %collective-permute-start.6 = (bf16[16,1536]{1,0:T(8,128)(2,1)S(1)}, bf16[16,1536]{1,0:T(8,128)(2,1)S(1)}, u32[]{:S(2)}, u32[]{:S(2)}) collective-permute-start(bf16[16,1536]{1,0:T(8,128)(2,1)S(1)} %fusion.2.refs_0_), channel_id=1, source_target_pairs={{0,4},{4,0},{8,12},{12,8},{1,5},{5,1},{9,13},{13,9},{2,6},{6,2},{1... | collective-permute-start | bytes 147464 | tf_op jit(solution)/shard_map/ppermute | solution.py:27
  62.0 12.9 %collective-permute-start.7 = (bf16[16,1536]{1,0:T(8,128)(2,1)S(1)}, bf16[16,1536]{1,0:T(8,128)(2,1)S(1)}, u32[]{:S(2)}, u32[]{:S(2)}) collective-permute-start(bf16[16,1536]{1,0:T(8,128)(2,1)S(1)} %collective-permute-done.5.refs_1_), channel_id=1, source_target_pairs={{0,4},{4,0},{8,12},{12,8},{1,5},{5,1},{9,13},{13,9},{2,6},{6,2},{1... | collective-permute-start | bytes 147464 | tf_op jit(solution)/shard_map/ppermute | solution.py:27
  79.2 6.9 %collective-permute-start.20 = (bf16[16,2048]{1,0:T(8,128)(2,1)S(1)}, bf16[16,2048]{1,0:T(8,128)(2,1)S(1)}, u32[]{:S(2)}, u32[]{:S(2)}) collective-permute-start(bf16[16,2048]{1,0:T(8,128)(2,1)S(1)} %get-tuple-element.24), channel_id=1, source_target_pairs={{0,3},{1,2},{2,1},{3,0},{4,7},{5,6},{6,5},{7,4},{8,11},{9,10},{10,... | collective-permute-start | bytes 196616 | tf_op jit(solution)/shard_map/ppermute | solution.py:27
  81.0 6.9 %collective-permute-start.19 = (bf16[16,2048]{1,0:T(8,128)(2,1)S(1)}, bf16[16,2048]{1,0:T(8,128)(2,1)S(1)}, u32[]{:S(2)}, u32[]{:S(2)}) collective-permute-start(bf16[16,2048]{1,0:T(8,128)(2,1)S(1)} %get-tuple-element.23), channel_id=1, source_target_pairs={{0,2},{1,3},{2,0},{3,1},{4,6},{5,7},{6,4},{7,5},{8,10},{9,11},{10,... | collective-permute-start | bytes 196616 | tf_op jit(solution)/shard_map/ppermute | solution.py:27
  81.0 6.9 %collective-permute-start.18 = (bf16[16,2048]{1,0:T(8,128)(2,1)S(1)}, bf16[16,2048]{1,0:T(8,128)(2,1)S(1)}, u32[]{:S(2)}, u32[]{:S(2)}) collective-permute-start(bf16[16,2048]{1,0:T(8,128)(2,1)S(1)} %get-tuple-element.22), channel_id=1, source_target_pairs={{0,1},{1,0},{2,3},{3,2},{4,5},{5,4},{6,7},{7,6},{8,9},{9,8},{10,11... | collective-permute-start | bytes 196616 | tf_op jit(solution)/shard_map/ppermute | solution.py:27

commit v2 on v0

v2 whole, which is shorter than its diff:
```python
import functools

import jax
import jax.numpy as jnp
from jax import lax
from jax.experimental import pallas as pl
from jax.experimental.pallas import tpu as pltpu
from jax.sharding import PartitionSpec as P

BLOCK = 128
STRIP = 6
UNITS = 5
VMEM_LIMIT = 4 * 2**20
DOWN = 2
HEAD = ("g0a", "g0b", "u0a", "u0b", "g1a", "g1b")
STEPS = (
    ("up", 0, ("u1a", "u1b", "g2a")),
    ("fetch", 0, ("g2b",)),
    ("join", 0, ()),
    ("up", 1, ("u2a", "u2b", "g3a")),
    ("fetch", 0, ("g3b",)),
    ("act", 0, ()),
    ("join", 1, ()),
    ("up", 2, ("u3a", "u3b", "g4a")),
    ("fetch", 0, ("g4b",)),
    ("act", 1, ()),
    ("join", 2, ()),
    ("up", 3, ("u4a", "u4b", "d0a")),
    ("fetch", 0, ("d0b",)),
    ("act", 2, ()),
    ("join", 3, ()),
    ("up", 4, ("d1a", "d1b", "d2a")),
    ("fetch", 0, ("d2b",)),
    ("act", 3, ()),
    ("join", 4, ()),
    ("down", 0, ("d3a", "d3b")),
    ("down", 1, ("d4a", "d4b")),
    ("act", 4, ()),
    ("down", 2, ()),
    ("down", 3, ()),
    ("last", 4, ()),
)

IN_HBM = pl.BlockSpec(memory_space=pltpu.HBM)
IN_VMEM = pl.BlockSpec(memory_space=pltpu.VMEM)
ANYWHERE = pl.BlockSpec(memory_space=pl.ANY)


def swap(value, axis, size, step):
    return lax.ppermute(value, axis, [(i, i ^ step) for i in range(size)])


def shaped(shape, dtype):
    return jax.ShapeDtypeStruct(shape, dtype)


def strip_of(blocks):
    return max(d for d in range(1, STRIP + 1) if blocks % d == 0)


def split_refs(refs, *counts):
    out, at = [], 0
    for count in counts:
        out.append(refs[at : at + count])
        at += count
    return out


def call(kernel, operands, outs, scratch, flops, read):
    specs, arrays = zip(*operands)
    return pl.pallas_call(
        kernel,
        out_shape=outs,
        in_specs=specs,
        out_specs=[IN_VMEM] * len(outs),
        scratch_shapes=scratch,
        cost_estimate=pl.CostEstimate(flops=flops, bytes_accessed=read, transcendentals=0),
        compiler_params=pltpu.CompilerParams(vmem_limit_bytes=VMEM_LIMIT),
    )(*arrays)


class Fetch:
    def __init__(self, plan):
        self.plan = plan

    def shapes(self):
        return [shaped(piece[3], jnp.bfloat16) for piece in self.plan]

    def bytes(self):
        return sum(2 * piece[3][0] * piece[3][1] for piece in self.plan)

    def sems(self):
        return pltpu.SemaphoreType.DMA((max(len(self.plan), 1),))

    def copies(self, sources, outs, sems):
        return [
            pltpu.make_async_copy(
                sources[which].at[pl.ds(row * BLOCK, shape[0]), pl.ds(col * BLOCK, shape[1])], out, sems.at[i]
            )
            for i, ((which, row, col, shape), out) in enumerate(zip(self.plan, outs))
        ]


def fetch_only(weights, fetch, after):
    def kernel(*refs):
        sources, _, outs, (sems,) = split_refs(refs, 3, len(after), len(fetch.plan), 1)
        copies = fetch.copies(sources, outs, sems)
        for copy in copies:
            copy.start()
        for copy in copies:
            copy.wait()

    return call(
        kernel,
        [(IN_HBM, a) for a in weights] + [(ANYWHERE, a) for a in after],
        fetch.shapes(),
        [fetch.sems()],
        0,
        fetch.bytes(),
    )


def spread_columns(scale, out):
    for c in range(scale.shape[1]):
        out[:, c * BLOCK : (c + 1) * BLOCK] = jnp.broadcast_to(scale[:, c : c + 1], (scale.shape[0], BLOCK))


def head(own, scales, down_scale, weights, fetch):
    count = len(scales)

    def kernel(*refs):
        (own_ref, *scale_refs), (down_ref,), sources, (own_out, *spread), (down_out,), outs, small, (sems, own_sems) = split_refs(
            refs, 1 + count, 1, 3, 1 + count, 1, len(fetch.plan), 1 + count, 2
        )
        copies = [
            pltpu.make_async_copy(ref, to, own_sems.at[i])
            for i, (ref, to) in enumerate(zip([*scale_refs, down_ref, own_ref], [*small, own_out]))
        ]
        copies += fetch.copies(sources, outs, sems)
        for copy in copies:
            copy.start()
        for copy in copies[: 2 + count]:
            copy.wait()
        for ref, out in zip(small[:count], spread):
            spread_columns(ref[...], out)
        spread_columns(jnp.transpose(small[count][...]), down_out)
        for copy in copies[2 + count :]:
            copy.wait()

    operands = [own, *scales, down_scale.T, *weights]
    outs = call(
        kernel,
        [(IN_HBM, pltpu.with_memory_space_constraint(a, pltpu.HBM)) for a in operands],
        [shaped(own.shape, own.dtype)]
        + [shaped((s.shape[0], s.shape[1] * BLOCK), jnp.float32) for s in [*scales, down_scale]]
        + fetch.shapes(),
        [pltpu.VMEM(s.shape, jnp.float32) for s in [*scales, down_scale.T]]
        + [fetch.sems(), pltpu.SemaphoreType.DMA((2 + count,))],
        0,
        fetch.bytes(),
    )
    return outs[0], outs[1 : 2 + count], outs[2 + count :]


def scaled_product(xs, weights, scale, row0, columns, scale_columns):
    total, k = None, 0
    for w in weights:
        for i in range(w.shape[0] // BLOCK):
            part = jnp.dot(
                xs[:, k * BLOCK : (k + 1) * BLOCK],
                w[i * BLOCK : (i + 1) * BLOCK, columns],
                preferred_element_type=jnp.float32,
            )
            part = part * scale[row0 + k : row0 + k + 1, scale_columns]
            total = part if total is None else total + part
            k += 1
    return total


def gate_up(rows, block0, gates, ups, scales, weights, fetch, after):
    ordered = len(rows) == 1
    depth, total = rows[0].shape[1], sum(r.shape[0] for r in rows)
    width = gates[0].shape[1]
    parts = len(gates)
    half = width // 2
    extra = 0 if ordered else 1
    strip = strip_of(half // BLOCK)
    per = half // BLOCK // strip

    def kernel(*refs):
        row_refs, gate_w, up_w, (gate_s, up_s), sources, _, (keep, send), xs_out, outs, (sems,) = split_refs(
            refs, len(rows), parts, parts, 2, 3, len(after), 2, extra, len(fetch.plan), 1
        )
        copies = fetch.copies(sources, outs, sems)
        for copy in copies:
            copy.start()
        xs = row_refs[0]
        if not ordered:
            xs = xs_out[0]
            at = 0
            for ref in row_refs:
                xs[at : at + ref.shape[0], :] = ref[...]
                at += ref.shape[0]
        core = lax.rem(lax.axis_index("gx"), 2)

        def body(step, carry):
            slot, within = step // per, lax.rem(step, per)
            first = lax.rem(slot + core, 2) * (half // BLOCK) + within * strip
            columns = pl.ds(pl.multiple_of(first * BLOCK, BLOCK), strip * BLOCK)
            for which, (w, s) in enumerate(((gate_w, gate_s), (up_w, up_s))):
                scale_columns = pl.ds(pl.multiple_of((block0 + first) * BLOCK, BLOCK), strip * BLOCK)
                value = scaled_product(xs, w, s, 0, columns, scale_columns)
                at = pl.ds(pl.multiple_of(which * half + within * strip * BLOCK, BLOCK), strip * BLOCK)

                @pl.when(slot == 0)
                def _():
                    keep[:, at] = value

                @pl.when(slot == 1)
                def _():
                    send[:, at] = value.astype(send.dtype)

            return carry

        lax.fori_loop(0, 2 * per, body, 0)
        for copy in copies:
            copy.wait()

    outs = call(
        kernel,
        [(IN_VMEM, a) for a in [*rows, *gates, *ups, *scales]]
        + [(IN_HBM, a) for a in weights]
        + [(ANYWHERE, a) for a in after],
        [shaped((total, width), jnp.float32), shaped((total, width), jnp.bfloat16)]
        + [shaped((total, depth), jnp.bfloat16)] * extra
        + fetch.shapes(),
        [fetch.sems()],
        4 * total * depth * width,
        4 * depth * width + fetch.bytes(),
    )
    return outs[0], outs[1], outs[2 : 2 + extra], outs[2 + extra :]


def by_strips(blocks, work):
    strip = strip_of(blocks)

    def body(step, carry):
        work(pl.multiple_of(step * strip * BLOCK, BLOCK), strip * BLOCK)
        return carry

    lax.fori_loop(0, blocks // strip, body, 0)


def join(keep, got, after):
    rows, width = keep.shape

    def kernel(keep_ref, got_ref, *rest):
        total_ref, send_ref = rest[len(after) :]

        def work(left, size):
            at = pl.ds(left, size)
            total = keep_ref[:, at] + got_ref[:, at].astype(jnp.float32)
            total_ref[:, at] = total
            send_ref[:, at] = total.astype(send_ref.dtype)

        by_strips(width // BLOCK, work)

    return call(
        kernel,
        [(IN_VMEM, keep), (IN_VMEM, got)] + [(ANYWHERE, a) for a in after],
        [shaped((rows, width), jnp.float32), shaped((rows, width), jnp.bfloat16)],
        [],
        rows * width,
        12 * rows * width,
    )


def activate(keep, got, after):
    rows, middle = keep.shape[0], keep.shape[1] // 2

    def kernel(keep_ref, got_ref, *rest):
        out = rest[-1]

        def work(left, size):
            gate_at, up_at = pl.ds(left, size), pl.ds(pl.multiple_of(middle + left, BLOCK), size)
            gate = keep_ref[:, gate_at] + got_ref[:, gate_at].astype(jnp.float32)
            up = keep_ref[:, up_at] + got_ref[:, up_at].astype(jnp.float32)
            out[:, gate_at] = (jax.nn.silu(gate) * up).astype(out.dtype)

        by_strips(middle // BLOCK, work)

    return call(
        kernel,
        [(IN_VMEM, keep), (IN_VMEM, got)] + [(ANYWHERE, a) for a in after],
        [shaped((rows, middle), jnp.bfloat16)],
        [],
        8 * rows * middle,
        14 * rows * middle,
    )[0]


def down(gy, own, other, prior, block0, units, scale, weights, fetch, after, last):
    total, half = own.shape
    depth, width = sum(u.shape[0] for u in units), units[0].shape[1]
    per = total // gy
    if last:
        result = [shaped((per, width), jnp.float32 if r == 0 else jnp.bfloat16) for r in range(gy)]
    else:
        result = [shaped((total, width), jnp.float32)]
    before = [] if prior is None else [prior]
    strip = strip_of(width // BLOCK)

    def kernel(*refs):
        (own_ref, other_ref), befores, w, (scale_ref,), sources, _, results, outs, (xs, sems) = split_refs(
            refs, 2, len(before), len(units), 1, 3, len(after), len(result), len(fetch.plan), 2
        )
        copies = fetch.copies(sources, outs, sems)
        for copy in copies:
            copy.start()
        core = lax.rem(lax.axis_index("gx"), 2)
        for slot, ref in enumerate((own_ref, other_ref)):
            xs[:, pl.ds(pl.multiple_of(lax.rem(core + slot, 2) * half, BLOCK), half)] = ref[...]

        def body(step, carry):
            columns = pl.ds(pl.multiple_of(step * strip * BLOCK, BLOCK), strip * BLOCK)
            value = scaled_product(xs, w, scale_ref, block0, columns, columns)
            if befores:
                value = value + befores[0][:, columns]
            if last:
                for r, out in enumerate(results):
                    out[:, columns] = value[r * per : (r + 1) * per].astype(out.dtype)
            else:
                results[0][:, columns] = value
            return carry

        lax.fori_loop(0, width // BLOCK // strip, body, 0)
        for copy in copies:
            copy.wait()

    outs = call(
        kernel,
        [(IN_VMEM, a) for a in [own, other, *before, *units, scale]]
        + [(IN_HBM, a) for a in weights]
        + [(ANYWHERE, a) for a in after],
        result + fetch.shapes(),
        [pltpu.VMEM((total, depth), jnp.bfloat16), fetch.sems()],
        2 * total * depth * width,
        2 * depth * width + fetch.bytes(),
    )
    return outs[: len(result)], outs[len(result) :]


def body(gx, gy, activations, gate_q, gate_s, up_q, up_s, down_q, down_s):
    weights = tuple(pltpu.with_memory_space_constraint(w, pltpu.HBM) for w in (gate_q, up_q, down_q))
    depth, width = gate_q.shape[0], down_q.shape[1]
    blocks = gate_q.shape[1] // BLOCK
    at = [2 * round(blocks / 2 * i / UNITS) for i in range(UNITS + 1)]
    later = [1 << k for k in range(1, gx.bit_length() - 1)]

    def planned(names):
        out = []
        for name in names:
            kind, unit, part = "gud".index(name[0]), int(name[1:-1]), "ab".index(name[-1])
            first, count = at[unit], at[unit + 1] - at[unit]
            if kind == DOWN:
                cut = count // 2
                first, count = (first, cut) if part == 0 else (first + cut, count - cut)
                out.append((kind, first, 0, (count * BLOCK, width)))
            else:
                cut = depth // BLOCK // 2
                low, high = (0, cut) if part == 0 else (cut, depth // BLOCK)
                out.append((kind, low, first, ((high - low) * BLOCK, count * BLOCK)))
        return Fetch(out)

    def pieces(letter, unit):
        return [held[f"{letter}{unit}{part}"] for part in "ab"]

    rows = [activations] + [swap(activations, "gy", gy, r) for r in range(1, gy)]
    rows[0], (*scales, down_s), arrays = head(activations, (gate_s, up_s), down_s, weights, planned(HEAD))
    held = dict(zip(HEAD, arrays))

    sums, hidden, total, after = {}, {}, None, []
    for op, unit, names in STEPS:
        arrays = []
        if op == "up":
            keep, send, ordered, arrays = gate_up(
                rows, at[unit], pieces("g", unit), pieces("u", unit), scales, weights, planned(names), after
            )
            rows = list(ordered) or rows
            sums[unit] = (keep, swap(send, "gx", gx, 1))
            after = [keep]
        elif op == "join":
            for step in later:
                keep, send = join(*sums[unit], after)
                sums[unit] = (keep, swap(send, "gx", gx, step))
                after = [keep]
        elif op == "act":
            own = activate(*sums[unit], after)
            hidden[unit] = (own, swap(own, "gx", gx, 1))
            after = [own]
        elif op == "fetch":
            arrays = fetch_only(weights, planned(names), after)
            after = [arrays[0]]
        else:
            outs, arrays = down(
                gy,
                *hidden[unit],
                total,
                at[unit],
                pieces("d", unit),
                down_s,
                weights,
                planned(names),
                after,
                op == "last",
            )
            total = outs[0]
            after = [total]
        held.update(zip(names, arrays))
    for r in range(1, gy):
        total = total + swap(outs[r], "gy", gy, r).astype(jnp.float32)
    return total.astype(jnp.bfloat16)


def solution(mesh):
    placed = (
        P(("groups", "gy"), "gx"),
        P("gx", "gy"),
        P("gx", "gy"),
        P("gx", "gy"),
        P("gx", "gy"),
        P("gy", "gx"),
        P("gy", "gx"),
    )
    return jax.shard_map(
        functools.partial(body, mesh.shape["gx"], mesh.shape["gy"]),
        mesh=mesh,
        in_specs=placed,
        out_specs=P(("groups", "gy"), "gx"),
        check_vma=False,
    )
```

time: 195 us -> 73.4 us (0.38)
  other arithmetic: 71.2 us -> 0.66 us
  Pallas kernels: 0 us -> 46.2 us
  matrix products: 39.1 us -> 0 us
  waiting for transfers between devices: 43.3 us -> 6.8 us
  blocking collectives: 25.1 us -> 0 us
  starting transfers between devices: 0.04 us -> 18.2 us
  between operations: 13.5 us -> 0.32 us
    convert_element_type x5 -> x1, other arithmetic: 69 us -> 0.66 us  [body(): return total.astype(jnp.bfloat16)]
    pallas_call x0 -> x26, Pallas kernels: none -> 46.2 us  [call(): pl.pallas_call(kernel, out_shape=outs, in_specs=specs, out_specs=[IN_VMEM...]
    reduce_scatter x2 -> x0, waiting for transfers between devices: 43.3 us -> none  [the longest x1 22.2 us: body(): lax.psum_scatter(jnp.dot(hidden, down_weight, preferred_element_type=jnp....]
    dot_general x3 -> x0, matrix products: 39.1 us -> none  [the longest x1 13.6 us: body(): jnp.dot(hidden, down_weight, preferred_element_type=jnp.float32)]
    all_gather x2 -> x0, blocking collectives: 25.1 us -> none  [the longest x1 15.8 us: body(): gathered_rows = lax.all_gather(activations, 'gy', axis=0, tiled=True)]
    ppermute x0 -> x21, starting transfers between devices: none -> 18.2 us  [swap(): return lax.ppermute(value, axis, [(i, i ^ step) for i in range(size)])]
    ppermute x0 -> x21, waiting for transfers between devices: none -> 6.8 us  [swap(): return lax.ppermute(value, axis, [(i, i ^ step) for i in range(size)])]
    concatenate x1 -> x0, other arithmetic: 2.13 us -> none  [body(): partials = jnp.concatenate([gate, up_values], axis=1)]
  transfers between devices with their start and end apart: 2 -> 21, of which waited for: 2 -> 4; matrix products, arithmetic and copies ran while one was open for 12% -> 0% of each run, Pallas kernels for 0% -> 55%
where the time goes in v2:
time: 73.4 us; the launch traced here: 73.1 us
  Pallas kernels  46.2 us (63%)
  starting transfers between devices  18.2 us (25%)
  waiting for transfers between devices  6.8 us (9%)
  local copies, waits for them, and re-layouts  0.9 us (1%)
    pallas_call x26, Pallas kernels, call(): pl.pallas_call(kernel, out_shape=outs, in_specs=specs, out_specs=[IN_VMEM...  46.2 us
    ppermute x21, starting transfers between devices, swap(): return lax.ppermute(value, axis, [(i, i ^ step) for i in range(size)])  18.2 us
    ppermute x21, waiting for transfers between devices, swap(): return lax.ppermute(value, axis, [(i, i ^ step) for i in range(size)])  6.8 us
  transfers between devices with their start and end apart: 21, of which 4 were waited for; matrix products, arithmetic and copies ran while one was open for 0% of the time, Pallas kernels for 55%

profile of v2, /device:TPU:0, one launch (start us, length us, event | category | flops | bytes accessed | tf_op | source)
XLA Modules:
  0.0 73.1 jit_solution(15018316604617215950)
XLA Ops:
  0.0 3.0 %collective-permute-start = (bf16[16,2048]{1,0:T(8,128)(2,1)}, bf16[16,2048]{1,0:T(8,128)(2,1)S(1)}, u32[]{:S(2)}, u32[]{:S(2)}) collective-permute-start(bf16[16,2048]{1,0:T(8,128)(2,1)} %refs_0_.6), channel_id=1, source_target_pairs={{0,1},{1,0},{2,3},{3,2},{4,5},{5,4},{6,7},{7,6},{8,9},{9,8},{10,11... | collective-permute-start | bytes 196616 | tf_op jit(solution)/shard_map/ppermute | solution.py:50
  3.0 2.6 %collective-permute-start.1 = (bf16[16,2048]{1,0:T(8,128)(2,1)}, bf16[16,2048]{1,0:T(8,128)(2,1)S(1)}, u32[]{:S(2)}, u32[]{:S(2)}) collective-permute-start(bf16[16,2048]{1,0:T(8,128)(2,1)} %refs_0_.6), channel_id=1, source_target_pairs={{0,2},{1,3},{2,0},{3,1},{4,6},{5,7},{6,4},{7,5},{8,10},{9,11},{10,... | collective-permute-start | bytes 196616 | tf_op jit(solution)/shard_map/ppermute | solution.py:50
  5.6 0.0 collective-permute-start.2
  5.6 6.7 %shard_map.73 = (bf16[16,2048]{1,0:T(8,128)(2,1)S(1)}, f32[16,7680]{1,0:T(8,128)S(1)}, f32[16,7680]{1,0:T(8,128)S(1)}, f32[60,2048]{1,0:T(8,128)S(1)}, bf16[1024...) custom-call(bf16[16,2048]{1,0:T(8,128)(2,1)} %refs_0_.6, ...), custom_call_target="tpu_custom_call" | custom-call | bytes 18874368 | tf_op jit(solution)/shard_map/pallas_call | solution.py:71
  12.3 0.0 collective-permute-done.refs_1_
  12.3 0.0 collective-permute-done.1.refs_2_
  12.3 3.8 %shard_map.74 = (f32[64,1536]{1,0:T(8,128)S(1)}, bf16[64,1536]{1,0:T(8,128)(2,1)S(1)}, bf16[64,2048]{1,0:T(8,128)(2,1)S(1)}, bf16[1024,1536]{1,0:T(8,128)(2,1)S(...) custom-call(bf16[16,2048]{1,0:T(8,128)(2,1)S(1)} %get-tuple-element.61.refs_0_, ...), custom_call_target="tpu_custom_call" | custom-call | flops 805306368 | bytes 22020096 | tf_op jit(solution)/shard_map/pallas_call | solution.py:71
  16.1 0.1 collective-permute-start.3
  16.2 1.9 %shard_map.75.rest_0_.refs_2_ = bf16[1024,1536]{1,0:T(8,128)(2,1)S(1)} custom-call(bf16[2048,7680]{1,0:T(8,128)(2,1)} %refs_6_.11, bf16[2048,7680]{1,0:T(8,128)(2,1)} %refs_7_.17, bf16[7680,2048]{1,0:T(8,128)(2,1)} %refs_8_.15, f32[64,1536]{1,0:T(8,128)S(1)} %get-tuple-element.70.refs_3_.keep_ref), custom_call_target="tpu_custom_call" | custom-call | bytes 3145728 | tf_op jit(solution)/shard_map/pallas_call | solution.py:71
  18.1 0.0 collective-permute-done.3.got_ref
  18.1 0.1 shard_map.76
  18.2 1.8 %collective-permute-start.5 = (bf16[64,1536]{1,0:T(8,128)(2,1)S(1)}, bf16[64,1536]{1,0:T(8,128)(2,1)S(1)}, u32[]{:S(2)}, u32[]{:S(2)}) collective-permute-start(bf16[64,1536]{1,0:T(8,128)(2,1)S(1)} %get-tuple-element.81), channel_id=1, source_target_pairs={{0,8},{4,12},{8,0},{12,4},{1,9},{5,13},{9,1},{13,5},{2,10},{6,14},... | collective-permute-start | bytes 589832 | tf_op jit(solution)/shard_map/ppermute | solution.py:50
  20.0 3.8 %shard_map.77 = (f32[64,1536]{1,0:T(8,128)S(1)}, bf16[64,1536]{1,0:T(8,128)(2,1)S(1)}, bf16[1024,1536]{1,0:T(8,128)(2,1)S(1)}, bf16[1024,1536]{1,0:T(8,128)(2,1)S(1)}, bf16[1024,1536]{1,0:T(8,128)(2,1)S(1)}) custom-call(bf16[64,2048]{1,0:T(8,128)(2,1)S(1)} %get-tuple-element.68.refs_0_, bf16[1024,1536]{1,0:T(8,128)(2,1)S(1)} %get-tuple-element.71.refs_1_, ...), custom_call_target="tpu_custom_call" | custom-call | flops 805306368 | bytes 22020096 | tf_op jit(solution)/shard_map/pallas_call | solution.py:71
  23.8 0.3 collective-permute-start.4
  24.0 1.9 %shard_map.78.rest_0_.refs_2_ = bf16[1024,1536]{1,0:T(8,128)(2,1)S(1)} custom-call(bf16[2048,7680]{1,0:T(8,128)(2,1)} %refs_6_.11, bf16[2048,7680]{1,0:T(8,128)(2,1)} %refs_7_.17, bf16[7680,2048]{1,0:T(8,128)(2,1)} %refs_8_.15, f32[64,1536]{1,0:T(8,128)S(1)} %get-tuple-element.79.refs_3_.keep_ref), custom_call_target="tpu_custom_call" | custom-call | bytes 3145728 | tf_op jit(solution)/shard_map/pallas_call | solution.py:71
  26.0 0.1 shard_map.79.rest_0_.refs_0_
  26.0 0.0 collective-permute-done.4.got_ref
  26.1 0.1 shard_map.80
  26.1 1.4 %collective-permute-start.7 = (bf16[64,1536]{1,0:T(8,128)(2,1)S(1)}, bf16[64,1536]{1,0:T(8,128)(2,1)S(1)}, u32[]{:S(2)}, u32[]{:S(2)}) collective-permute-start(bf16[64,1536]{1,0:T(8,128)(2,1)S(1)} %get-tuple-element.89), channel_id=1, source_target_pairs={{0,8},{4,12},{8,0},{12,4},{1,9},{5,13},{9,1},{13,5},{2,10},{6,14},... | collective-permute-start | bytes 589832 | tf_op jit(solution)/shard_map/ppermute | solution.py:50
  27.5 3.8 %shard_map.81 = (f32[64,1536]{1,0:T(8,128)S(1)}, bf16[64,1536]{1,0:T(8,128)(2,1)S(1)}, bf16[1024,1536]{1,0:T(8,128)(2,1)S(1)}, bf16[1024,1536]{1,0:T(8,128)(2,1)S(1)}, bf16[1024,1536]{1,0:T(8,128)(2,1)S(1)}) custom-call(bf16[64,2048]{1,0:T(8,128)(2,1)S(1)} %get-tuple-element.68.refs_0_, bf16[1024,1536]{1,0:T(8,128)(2,1)S(1)} %get-tuple-element.69.refs_1_, ...), custom_call_target="tpu_custom_call" | custom-call | flops 805306368 | bytes 22020096 | tf_op jit(solution)/shard_map/pallas_call | solution.py:71
  31.3 0.1 collective-permute-start.6
  31.4 1.9 %shard_map.82.rest_0_.refs_2_ = bf16[1024,1536]{1,0:T(8,128)(2,1)S(1)} custom-call(bf16[2048,7680]{1,0:T(8,128)(2,1)} %refs_6_.11, bf16[2048,7680]{1,0:T(8,128)(2,1)} %refs_7_.17, bf16[7680,2048]{1,0:T(8,128)(2,1)} %refs_8_.15, f32[64,1536]{1,0:T(8,128)S(1)} %get-tuple-element.84.refs_3_.keep_ref), custom_call_target="tpu_custom_call" | custom-call | bytes 3145728 | tf_op jit(solution)/shard_map/pallas_call | solution.py:71
  33.3 0.0 collective-permute-done.7.got_ref
  33.3 0.1 shard_map.83.rest_0_.refs_0_
  33.4 0.1 shard_map.84
  33.4 0.8 %collective-permute-start.9 = (bf16[64,1536]{1,0:T(8,128)(2,1)S(1)}, bf16[64,1536]{1,0:T(8,128)(2,1)S(1)}, u32[]{:S(2)}, u32[]{:S(2)}) collective-permute-start(bf16[64,1536]{1,0:T(8,128)(2,1)S(1)} %get-tuple-element.95), channel_id=1, source_target_pairs={{0,8},{4,12},{8,0},{12,4},{1,9},{5,13},{9,1},{13,5},{2,10},{6,14},... | collective-permute-start | bytes 589832 | tf_op jit(solution)/shard_map/ppermute | solution.py:50
  34.2 3.8 %shard_map.85 = (f32[64,1536]{1,0:T(8,128)S(1)}, bf16[64,1536]{1,0:T(8,128)(2,1)S(1)}, bf16[1024,1536]{1,0:T(8,128)(2,1)S(1)}, bf16[1024,1536]{1,0:T(8,128)(2,1)S(1)}, bf16[768,2048]{1,0:T(8,128)(2,1)S(1)}) custom-call(bf16[64,2048]{1,0:T(8,128)(2,1)S(1)} %get-tuple-element.68.refs_0_, bf16[1024,1536]{1,0:T(8,128)(2,1)S(1)} %get-tuple-element.85.refs_1_, ...), custom_call_target="tpu_custom_call" | custom-call | flops 805306368 | bytes 22020096 | tf_op jit(solution)/shard_map/pallas_call | solution.py:71
  38.0 0.3 collective-permute-start.8
  38.3 1.9 %shard_map.86.rest_0_.refs_3_ = bf16[768,2048]{1,0:T(8,128)(2,1)S(1)} custom-call(bf16[2048,7680]{1,0:T(8,128)(2,1)} %refs_6_.11, bf16[2048,7680]{1,0:T(8,128)(2,1)} %refs_7_.17, bf16[7680,2048]{1,0:T(8,128)(2,1)} %refs_8_.15, f32[64,1536]{1,0:T(8,128)S(1)} %get-tuple-element.93.refs_3_.keep_ref), custom_call_target="tpu_custom_call" | custom-call | bytes 3145728 | tf_op jit(solution)/shard_map/pallas_call | solution.py:71
  40.2 0.6 collective-permute-done.9.got_ref
  40.8 0.1 shard_map.87.rest_0_.refs_0_
  40.9 0.0 collective-permute-done.8.got_ref
  40.9 0.1 shard_map.88
  40.9 0.8 %collective-permute-start.11 = (bf16[64,1536]{1,0:T(8,128)(2,1)S(1)}, bf16[64,1536]{1,0:T(8,128)(2,1)S(1)}, u32[]{:S(2)}, u32[]{:S(2)}) collective-permute-start(bf16[64,1536]{1,0:T(8,128)(2,1)S(1)} %get-tuple-element.99), channel_id=1, source_target_pairs={{0,8},{4,12},{8,0},{12,4},{1,9},{5,13},{9,1},{13,5},{2,10},{6,14},... | collective-permute-start | bytes 589832 | tf_op jit(solution)/shard_map/ppermute | solution.py:50
  41.7 3.8 %shard_map.89 = (f32[64,1536]{1,0:T(8,128)S(1)}, bf16[64,1536]{1,0:T(8,128)(2,1)S(1)}, bf16[768,2048]{1,0:T(8,128)(2,1)S(1)}, bf16[768,2048]{1,0:T(8,128)(2,1)S(1)}, bf16[768,2048]{1,0:T(8,128)(2,1)S(1)}) custom-call(bf16[64,2048]{1,0:T(8,128)(2,1)S(1)} %get-tuple-element.68.refs_0_, bf16[1024,1536]{1,0:T(8,128)(2,1)S(1)} %get-tuple-element.83.refs_1_, ...), custom_call_target="tpu_custom_call" | custom-call | flops 805306368 | bytes 22020096 | tf_op jit(solution)/shard_map/pallas_call | solution.py:71
  45.5 0.1 collective-permute-start.10
  45.6 1.9 %shard_map.90.rest_0_.refs_4_ = bf16[768,2048]{1,0:T(8,128)(2,1)S(1)} custom-call(bf16[2048,7680]{1,0:T(8,128)(2,1)} %refs_6_.11, bf16[2048,7680]{1,0:T(8,128)(2,1)} %refs_7_.17, bf16[7680,2048]{1,0:T(8,128)(2,1)} %refs_8_.15, f32[64,1536]{1,0:T(8,128)S(1)} %get-tuple-element.97.refs_3_.keep_ref), custom_call_target="tpu_custom_call" | custom-call | bytes 3145728 | tf_op jit(solution)/shard_map/pallas_call | solution.py:71
  47.5 0.0 collective-permute-done.11.got_ref
  47.5 0.1 shard_map.91.rest_0_.refs_0_
  47.6 0.0 collective-permute-done.10.got_ref
  47.6 0.1 shard_map.92
  47.7 1.4 %collective-permute-start.12 = (bf16[64,1536]{1,0:T(8,128)(2,1)S(1)}, bf16[64,1536]{1,0:T(8,128)(2,1)S(1)}, u32[]{:S(2)}, u32[]{:S(2)}) collective-permute-start(bf16[64,1536]{1,0:T(8,128)(2,1)S(1)} %get-tuple-element.101), channel_id=1, source_target_pairs={{0,8},{4,12},{8,0},{12,4},{1,9},{5,13},{9,1},{13,5},{2,10},{6,14},... | collective-permute-start | bytes 589832 | tf_op jit(solution)/shard_map/ppermute | solution.py:50
  49.1 0.2 collective-permute-start.14
  49.2 0.3 collective-permute-start.13
  49.6 0.2 collective-permute-start.17
  49.8 0.3 collective-permute-start.16
  50.1 0.3 collective-permute-done.14.refs_1_
  50.4 0.9 %copy-done.1 = bf16[64,768]{1,0:T(8,128)(2,1)S(1)} copy-done((bf16[64,768]{1,0:T(8,128)(2,1)S(1)}, bf16[64,768]{1,0:T(8,128)(2,1)}, u32[]{:S(2)}) %copy-start.1) | copy-done | bytes 98328
  51.2 2.9 %shard_map.93 = (f32[64,2048]{1,0:T(8,128)S(1)}, bf16[768,2048]{1,0:T(8,128)(2,1)S(1)}, bf16[768,2048]{1,0:T(8,128)(2,1)S(1)}) custom-call(bf16[64,768]{1,0:T(8,128)(2,1)S(1)} %copy-done.1, bf16[64,768]{1,0:T(8,128)(2,1)S(1)} %collective-permute-done.14.refs_1_, bf16[768,2048]{1,0:T(8,128)(2,1)S(1)} %get-tuple-element.102.refs_2_, ...), custom_call_target="tpu_custom_call" | custom-call | flops 402653184 | bytes 12582912 | tf_op jit(solution)/shard_map/pallas_call | solution.py:71
  54.1 0.0 collective-permute-done.13.refs_1_
  54.1 2.9 %shard_map.94 = (f32[64,2048]{1,0:T(8,128)S(1)}, bf16[768,2048]{1,0:T(8,128)(2,1)S(1)}, bf16[768,2048]{1,0:T(8,128)(2,1)S(1)}) custom-call(bf16[64,768]{1,0:T(8,128)(2,1)S(1)} %shard_map.83.rest_0_.refs_0_, bf16[64,768]{1,0:T(8,128)(2,1)S(1)} %collective-permute-done.13.refs_1_, f32[64,2048]{1,0:T(8,128)S(1)} %get-tuple-element.104.refs_2_.refs_9_, ...), custom_call_target="tpu_custom_call" | custom-call | flops 402653184 | bytes 12582912 | tf_op jit(solution)/shard_map/pallas_call | solution.py:71
  57.0 0.0 collective-permute-done.12.got_ref
  57.0 0.1 shard_map.95.refs_9_.refs_0_
  57.1 0.3 collective-permute-start.15
  57.3 0.0 collective-permute-done.17.refs_1_
  57.3 1.6 %shard_map.96.refs_2_.refs_9_ = f32[64,2048]{1,0:T(8,128)S(1)} custom-call(bf16[64,768]{1,0:T(8,128)(2,1)S(1)} %shard_map.87.rest_0_.refs_0_, bf16[64,768]{1,0:T(8,128)(2,1)S(1)} %collective-permute-done.17.refs_1_, f32[64,2048]{1,0:T(8,128)S(1)} %get-tuple-element.107.rest_0_.refs_2_, bf16[768,2048]{1,0:T(8,128)(2,1)S(1)} %get-tuple-element.108.refs_3_, ...), custom_call_target="tpu_custom_call" | custom-call | flops 402653184 | bytes 6291456 | tf_op jit(solution)/shard_map/pallas_call | solution.py:71
  58.9 1.6 %shard_map.97.refs_2_.refs_9_ = f32[64,2048]{1,0:T(8,128)S(1)} custom-call(bf16[64,768]{1,0:T(8,128)(2,1)S(1)} %shard_map.91.rest_0_.refs_0_, bf16[64,768]{1,0:T(8,128)(2,1)S(1)} %collective-permute-done.16.refs_1_, f32[64,2048]{1,0:T(8,128)S(1)} %shard_map.96.refs_2_.refs_9_, bf16[768,2048]{1,0:T(8,128)(2,1)S(1)} %get-tuple-element.109.refs_3_, ...), custom_call_target="tpu_custom_call" | custom-call | flops 402653184 | bytes 6291456 | tf_op jit(solution)/shard_map/pallas_call | solution.py:71
  60.5 1.6 %shard_map.98 = (f32[16,2048]{1,0:T(8,128)S(1)}, bf16[16,2048]{1,0:T(8,128)(2,1)S(1)}, bf16[16,2048]{1,0:T(8,128)(2,1)S(1)}, bf16[16,2048]{1,0:T(8,128)(2,1)S(1)}) custom-call(bf16[64,768]{1,0:T(8,128)(2,1)S(1)} %shard_map.95.refs_9_.refs_0_, bf16[64,768]{1,0:T(8,128)(2,1)S(1)} %collective-permute-done.15.refs_1_, f32[64,2048]{1,0:T(8,128)S(1)} %shard_map.97.refs_2_.refs_9_, ...), custom_call_target="tpu_custom_call" | custom-call | flops 402653184 | bytes 6291456 | tf_op jit(solution)/shard_map/pallas_call | solution.py:71
  62.1 0.7 collective-permute-start.18
  62.9 3.5 %collective-permute-start.19 = (bf16[16,2048]{1,0:T(8,128)(2,1)S(1)}, bf16[16,2048]{1,0:T(8,128)(2,1)S(1)}, u32[]{:S(2)}, u32[]{:S(2)}) collective-permute-start(bf16[16,2048]{1,0:T(8,128)(2,1)S(1)} %get-tuple-element.115), channel_id=1, source_target_pairs={{0,2},{1,3},{2,0},{3,1},{4,6},{5,7},{6,4},{7,5},{8,10},{9,11},{10,... | collective-permute-start | bytes 196616 | tf_op jit(solution)/shard_map/ppermute | solution.py:50
  66.3 0.3 collective-permute-start.20
  66.6 3.8 %collective-permute-done.19 = bf16[16,2048]{1,0:T(8,128)(2,1)S(1)} collective-permute-done((bf16[16,2048]{1,0:T(8,128)(2,1)S(1)}, bf16[16,2048]{1,0:T(8,128)(2,1)S(1)}, u32[]{:S(2)}, u32[]{:S(2)}) %collective-permute-start.19) | collective-permute-done | bytes 65568 | tf_op jit(solution)/shard_map/ppermute | solution.py:50
  70.4 2.1 %collective-permute-done.20 = bf16[16,2048]{1,0:T(8,128)(2,1)S(1)} collective-permute-done((bf16[16,2048]{1,0:T(8,128)(2,1)S(1)}, bf16[16,2048]{1,0:T(8,128)(2,1)S(1)}, u32[]{:S(2)}, u32[]{:S(2)}) %collective-permute-start.20) | collective-permute-done | bytes 65568 | tf_op jit(solution)/shard_map/ppermute | solution.py:50
  72.5 0.7 add_convert_fusion
  (9 shorter events, 0.0 us)
Async XLA Ops:
  0.0 12.3 %collective-permute-start = (bf16[16,2048]{1,0:T(8,128)(2,1)}, bf16[16,2048]{1,0:T(8,128)(2,1)S(1)}, u32[]{:S(2)}, u32[]{:S(2)}) collective-permute-start(bf16[16,2048]{1,0:T(8,128)(2,1)} %refs_0_.6), channel_id=1, source_target_pairs={{0,1},{1,0},{2,3},{3,2},{4,5},{5,4},{6,7},{7,6},{8,9},{9,8},{10,11... | collective-permute-start | bytes 196616 | tf_op jit(solution)/shard_map/ppermute | solution.py:50
  3.0 9.3 %collective-permute-start.1 = (bf16[16,2048]{1,0:T(8,128)(2,1)}, bf16[16,2048]{1,0:T(8,128)(2,1)S(1)}, u32[]{:S(2)}, u32[]{:S(2)}) collective-permute-start(bf16[16,2048]{1,0:T(8,128)(2,1)} %refs_0_.6), channel_id=1, source_target_pairs={{0,2},{1,3},{2,0},{3,1},{4,6},{5,7},{6,4},{7,5},{8,10},{9,11},{10,... | collective-permute-start | bytes 196616 | tf_op jit(solution)/shard_map/ppermute | solution.py:50
  5.6 6.7 %collective-permute-start.2 = (bf16[16,2048]{1,0:T(8,128)(2,1)}, bf16[16,2048]{1,0:T(8,128)(2,1)S(1)}, u32[]{:S(2)}, u32[]{:S(2)}) collective-permute-start(bf16[16,2048]{1,0:T(8,128)(2,1)} %refs_0_.6), channel_id=1, source_target_pairs={{0,3},{1,2},{2,1},{3,0},{4,7},{5,6},{6,5},{7,4},{8,11},{9,10},{10,... | collective-permute-start | bytes 196616 | tf_op jit(solution)/shard_map/ppermute | solution.py:50
  16.1 2.0 %collective-permute-start.3 = (bf16[64,1536]{1,0:T(8,128)(2,1)S(1)}, bf16[64,1536]{1,0:T(8,128)(2,1)S(1)}, u32[]{:S(2)}, u32[]{:S(2)}) collective-permute-start(bf16[64,1536]{1,0:T(8,128)(2,1)S(1)} %get-tuple-element.75), channel_id=1, source_target_pairs={{0,4},{4,0},{8,12},{12,8},{1,5},{5,1},{9,13},{13,9},{2,6},{6,2},{1... | collective-permute-start | bytes 589832 | tf_op jit(solution)/shard_map/ppermute | solution.py:50
  18.2 7.8 %collective-permute-start.5 = (bf16[64,1536]{1,0:T(8,128)(2,1)S(1)}, bf16[64,1536]{1,0:T(8,128)(2,1)S(1)}, u32[]{:S(2)}, u32[]{:S(2)}) collective-permute-start(bf16[64,1536]{1,0:T(8,128)(2,1)S(1)} %get-tuple-element.81), channel_id=1, source_target_pairs={{0,8},{4,12},{8,0},{12,4},{1,9},{5,13},{9,1},{13,5},{2,10},{6,14},... | collective-permute-start | bytes 589832 | tf_op jit(solution)/shard_map/ppermute | solution.py:50
  23.8 2.3 %collective-permute-start.4 = (bf16[64,1536]{1,0:T(8,128)(2,1)S(1)}, bf16[64,1536]{1,0:T(8,128)(2,1)S(1)}, u32[]{:S(2)}, u32[]{:S(2)}) collective-permute-start(bf16[64,1536]{1,0:T(8,128)(2,1)S(1)} %get-tuple-element.80), channel_id=1, source_target_pairs={{0,4},{4,0},{8,12},{12,8},{1,5},{5,1},{9,13},{13,9},{2,6},{6,2},{1... | collective-permute-start | bytes 589832 | tf_op jit(solution)/shard_map/ppermute | solution.py:50
  26.0 23.0 %copy-start = (bf16[64,768]{1,0:T(8,128)(2,1)}, bf16[64,768]{1,0:T(8,128)(2,1)S(1)}, u32[]{:S(2)}) copy-start(bf16[64,768]{1,0:T(8,128)(2,1)S(1)} %shard_map.79.rest_0_.refs_0_) | copy-start | bytes 294916
  26.1 7.2 %collective-permute-start.7 = (bf16[64,1536]{1,0:T(8,128)(2,1)S(1)}, bf16[64,1536]{1,0:T(8,128)(2,1)S(1)}, u32[]{:S(2)}, u32[]{:S(2)}) collective-permute-start(bf16[64,1536]{1,0:T(8,128)(2,1)S(1)} %get-tuple-element.89), channel_id=1, source_target_pairs={{0,8},{4,12},{8,0},{12,4},{1,9},{5,13},{9,1},{13,5},{2,10},{6,14},... | collective-permute-start | bytes 589832 | tf_op jit(solution)/shard_map/ppermute | solution.py:50
  31.3 2.1 %collective-permute-start.6 = (bf16[64,1536]{1,0:T(8,128)(2,1)S(1)}, bf16[64,1536]{1,0:T(8,128)(2,1)S(1)}, u32[]{:S(2)}, u32[]{:S(2)}) collective-permute-start(bf16[64,1536]{1,0:T(8,128)(2,1)S(1)} %get-tuple-element.88), channel_id=1, source_target_pairs={{0,4},{4,0},{8,12},{12,8},{1,5},{5,1},{9,13},{13,9},{2,6},{6,2},{1... | collective-permute-start | bytes 589832 | tf_op jit(solution)/shard_map/ppermute | solution.py:50
  33.4 7.4 %collective-permute-start.9 = (bf16[64,1536]{1,0:T(8,128)(2,1)S(1)}, bf16[64,1536]{1,0:T(8,128)(2,1)S(1)}, u32[]{:S(2)}, u32[]{:S(2)}) collective-permute-start(bf16[64,1536]{1,0:T(8,128)(2,1)S(1)} %get-tuple-element.95), channel_id=1, source_target_pairs={{0,8},{4,12},{8,0},{12,4},{1,9},{5,13},{9,1},{13,5},{2,10},{6,14},... | collective-permute-start | bytes 589832 | tf_op jit(solution)/shard_map/ppermute | solution.py:50
  38.0 2.8 %collective-permute-start.8 = (bf16[64,1536]{1,0:T(8,128)(2,1)S(1)}, bf16[64,1536]{1,0:T(8,128)(2,1)S(1)}, u32[]{:S(2)}, u32[]{:S(2)}) collective-permute-start(bf16[64,1536]{1,0:T(8,128)(2,1)S(1)} %get-tuple-element.94), channel_id=1, source_target_pairs={{0,4},{4,0},{8,12},{12,8},{1,5},{5,1},{9,13},{13,9},{2,6},{6,2},{1... | collective-permute-start | bytes 589832 | tf_op jit(solution)/shard_map/ppermute | solution.py:50
  40.9 6.6 %collective-permute-start.11 = (bf16[64,1536]{1,0:T(8,128)(2,1)S(1)}, bf16[64,1536]{1,0:T(8,128)(2,1)S(1)}, u32[]{:S(2)}, u32[]{:S(2)}) collective-permute-start(bf16[64,1536]{1,0:T(8,128)(2,1)S(1)} %get-tuple-element.99), channel_id=1, source_target_pairs={{0,8},{4,12},{8,0},{12,4},{1,9},{5,13},{9,1},{13,5},{2,10},{6,14},... | collective-permute-start | bytes 589832 | tf_op jit(solution)/shard_map/ppermute | solution.py:50
  45.5 2.1 %collective-permute-start.10 = (bf16[64,1536]{1,0:T(8,128)(2,1)S(1)}, bf16[64,1536]{1,0:T(8,128)(2,1)S(1)}, u32[]{:S(2)}, u32[]{:S(2)}) collective-permute-start(bf16[64,1536]{1,0:T(8,128)(2,1)S(1)} %get-tuple-element.98), channel_id=1, source_target_pairs={{0,4},{4,0},{8,12},{12,8},{1,5},{5,1},{9,13},{13,9},{2,6},{6,2},{1... | collective-permute-start | bytes 589832 | tf_op jit(solution)/shard_map/ppermute | solution.py:50
  47.7 9.3 %collective-permute-start.12 = (bf16[64,1536]{1,0:T(8,128)(2,1)S(1)}, bf16[64,1536]{1,0:T(8,128)(2,1)S(1)}, u32[]{:S(2)}, u32[]{:S(2)}) collective-permute-start(bf16[64,1536]{1,0:T(8,128)(2,1)S(1)} %get-tuple-element.101), channel_id=1, source_target_pairs={{0,8},{4,12},{8,0},{12,4},{1,9},{5,13},{9,1},{13,5},{2,10},{6,14},... | collective-permute-start | bytes 589832 | tf_op jit(solution)/shard_map/ppermute | solution.py:50
  49.1 1.3 %collective-permute-start.14 = (bf16[64,768]{1,0:T(8,128)(2,1)S(1)}, bf16[64,768]{1,0:T(8,128)(2,1)S(1)}, u32[]{:S(2)}, u32[]{:S(2)}) collective-permute-start(bf16[64,768]{1,0:T(8,128)(2,1)S(1)} %shard_map.79.rest_0_.refs_0_), channel_id=1, source_target_pairs={{0,4},{4,0},{8,12},{12,8},{1,5},{5,1},{9,13},{13,9},{2,6},{6,2},{1... | collective-permute-start | bytes 294920 | tf_op jit(solution)/shard_map/ppermute | solution.py:50
  49.2 4.9 %collective-permute-start.13 = (bf16[64,768]{1,0:T(8,128)(2,1)S(1)}, bf16[64,768]{1,0:T(8,128)(2,1)S(1)}, u32[]{:S(2)}, u32[]{:S(2)}) collective-permute-start(bf16[64,768]{1,0:T(8,128)(2,1)S(1)} %shard_map.83.rest_0_.refs_0_), channel_id=1, source_target_pairs={{0,4},{4,0},{8,12},{12,8},{1,5},{5,1},{9,13},{13,9},{2,6},{6,2},{1... | collective-permute-start | bytes 294920 | tf_op jit(solution)/shard_map/ppermute | solution.py:50
  49.6 7.8 %collective-permute-start.17 = (bf16[64,768]{1,0:T(8,128)(2,1)S(1)}, bf16[64,768]{1,0:T(8,128)(2,1)S(1)}, u32[]{:S(2)}, u32[]{:S(2)}) collective-permute-start(bf16[64,768]{1,0:T(8,128)(2,1)S(1)} %shard_map.87.rest_0_.refs_0_), channel_id=1, source_target_pairs={{0,4},{4,0},{8,12},{12,8},{1,5},{5,1},{9,13},{13,9},{2,6},{6,2},{1... | collective-permute-start | bytes 294920 | tf_op jit(solution)/shard_map/ppermute | solution.py:50
  49.8 9.2 %collective-permute-start.16 = (bf16[64,768]{1,0:T(8,128)(2,1)S(1)}, bf16[64,768]{1,0:T(8,128)(2,1)S(1)}, u32[]{:S(2)}, u32[]{:S(2)}) collective-permute-start(bf16[64,768]{1,0:T(8,128)(2,1)S(1)} %shard_map.91.rest_0_.refs_0_), channel_id=1, source_target_pairs={{0,4},{4,0},{8,12},{12,8},{1,5},{5,1},{9,13},{13,9},{2,6},{6,2},{1... | collective-permute-start | bytes 294920 | tf_op jit(solution)/shard_map/ppermute | solution.py:50
  50.4 0.9 %copy-start.1 = (bf16[64,768]{1,0:T(8,128)(2,1)S(1)}, bf16[64,768]{1,0:T(8,128)(2,1)}, u32[]{:S(2)}) copy-start(bf16[64,768]{1,0:T(8,128)(2,1)} %copy-done) | copy-start | bytes 294916
  57.1 3.5 %collective-permute-start.15 = (bf16[64,768]{1,0:T(8,128)(2,1)S(1)}, bf16[64,768]{1,0:T(8,128)(2,1)S(1)}, u32[]{:S(2)}, u32[]{:S(2)}) collective-permute-start(bf16[64,768]{1,0:T(8,128)(2,1)S(1)} %shard_map.95.refs_9_.refs_0_), channel_id=1, source_target_pairs={{0,4},{4,0},{8,12},{12,8},{1,5},{5,1},{9,13},{13,9},{2,6},{6,2},{1... | collective-permute-start | bytes 294920 | tf_op jit(solution)/shard_map/ppermute | solution.py:50
  62.1 4.5 %collective-permute-start.18 = (bf16[16,2048]{1,0:T(8,128)(2,1)S(1)}, bf16[16,2048]{1,0:T(8,128)(2,1)S(1)}, u32[]{:S(2)}, u32[]{:S(2)}) collective-permute-start(bf16[16,2048]{1,0:T(8,128)(2,1)S(1)} %get-tuple-element.114), channel_id=1, source_target_pairs={{0,1},{1,0},{2,3},{3,2},{4,5},{5,4},{6,7},{7,6},{8,9},{9,8},{10,11... | collective-permute-start | bytes 196616 | tf_op jit(solution)/shard_map/ppermute | solution.py:50
  62.9 7.5 %collective-permute-start.19 = (bf16[16,2048]{1,0:T(8,128)(2,1)S(1)}, bf16[16,2048]{1,0:T(8,128)(2,1)S(1)}, u32[]{:S(2)}, u32[]{:S(2)}) collective-permute-start(bf16[16,2048]{1,0:T(8,128)(2,1)S(1)} %get-tuple-element.115), channel_id=1, source_target_pairs={{0,2},{1,3},{2,0},{3,1},{4,6},{5,7},{6,4},{7,5},{8,10},{9,11},{10,... | collective-permute-start | bytes 196616 | tf_op jit(solution)/shard_map/ppermute | solution.py:50
  66.3 6.1 %collective-permute-start.20 = (bf16[16,2048]{1,0:T(8,128)(2,1)S(1)}, bf16[16,2048]{1,0:T(8,128)(2,1)S(1)}, u32[]{:S(2)}, u32[]{:S(2)}) collective-permute-start(bf16[16,2048]{1,0:T(8,128)(2,1)S(1)} %get-tuple-element.116), channel_id=1, source_target_pairs={{0,3},{1,2},{2,1},{3,0},{4,7},{5,6},{6,5},{7,4},{8,11},{9,10},{10,... | collective-permute-start | bytes 196616 | tf_op jit(solution)/shard_map/ppermute | solution.py:50

commit v3 on v2

--- a/solution.py
+++ b/solution.py
@@ -8,37 +8,28 @@
 from jax.sharding import PartitionSpec as P
 
 BLOCK = 128
-STRIP = 6
-UNITS = 5
+STRIP = 8
 VMEM_LIMIT = 4 * 2**20
 DOWN = 2
-HEAD = ("g0a", "g0b", "u0a", "u0b", "g1a", "g1b")
+SPLIT = (24, 20, 16)
+PARTS = 8
+HEAD = 268
 STEPS = (
-    ("up", 0, ("u1a", "u1b", "g2a")),
-    ("fetch", 0, ("g2b",)),
-    ("join", 0, ()),
-    ("up", 1, ("u2a", "u2b", "g3a")),
-    ("fetch", 0, ("g3b",)),
-    ("act", 0, ()),
-    ("join", 1, ()),
-    ("up", 2, ("u3a", "u3b", "g4a")),
-    ("fetch", 0, ("g4b",)),
-    ("act", 1, ()),
-    ("join", 2, ()),
-    ("up", 3, ("u4a", "u4b", "d0a")),
-    ("fetch", 0, ("d0b",)),
-    ("act", 2, ()),
-    ("join", 3, ()),
-    ("up", 4, ("d1a", "d1b", "d2a")),
-    ("fetch", 0, ("d2b",)),
-    ("act", 3, ()),
-    ("join", 4, ()),
-    ("down", 0, ("d3a", "d3b")),
-    ("down", 1, ("d4a", "d4b")),
-    ("act", 4, ()),
-    ("down", 2, ()),
-    ("down", 3, ()),
-    ("last", 4, ()),
+    ("up", 0, 165),
+    ("fetch", 0, 60),
+    ("join", 0, 0),
+    ("up", 1, 150),
+    ("fetch", 0, 65),
+    ("join", 1, 0),
+    ("act", 0, 0),
+    ("up", 2, 100),
+    ("fetch", 0, 60),
+    ("join", 2, 0),
+    ("act", 1, 0),
+    ("down", 0, 70),
+    ("down", 1, 70),
+    ("act", 2, 0),
+    ("last", 2, 0),
 )
 
 IN_HBM = pl.BlockSpec(memory_space=pltpu.HBM)
@@ -354,52 +345,76 @@
     weights = tuple(pltpu.with_memory_space_constraint(w, pltpu.HBM) for w in (gate_q, up_q, down_q))
     depth, width = gate_q.shape[0], down_q.shape[1]
     blocks = gate_q.shape[1] // BLOCK
-    at = [2 * round(blocks / 2 * i / UNITS) for i in range(UNITS + 1)]
+    at = [2 * round(blocks / 2 * sum(SPLIT[:i]) / sum(SPLIT)) for i in range(len(SPLIT) + 1)]
     later = [1 << k for k in range(1, gx.bit_length() - 1)]
 
-    def planned(names):
-        out = []
-        for name in names:
-            kind, unit, part = "gud".index(name[0]), int(name[1:-1]), "ab".index(name[-1])
-            first, count = at[unit], at[unit + 1] - at[unit]
-            if kind == DOWN:
-                cut = count // 2
-                first, count = (first, cut) if part == 0 else (first + cut, count - cut)
-                out.append((kind, first, 0, (count * BLOCK, width)))
-            else:
-                cut = depth // BLOCK // 2
-                low, high = (0, cut) if part == 0 else (cut, depth // BLOCK)
-                out.append((kind, low, first, ((high - low) * BLOCK, count * BLOCK)))
-        return Fetch(out)
-
-    def pieces(letter, unit):
-        return [held[f"{letter}{unit}{part}"] for part in "ab"]
+    def piece_of(kind, unit, part):
+        first, count = at[unit], at[unit + 1] - at[unit]
+        total = count if kind == DOWN else depth // BLOCK
+        low, high = total * part // PARTS, total * (part + 1) // PARTS
+        if kind == DOWN:
+            return kind, first + low, 0, ((high - low) * BLOCK, width)
+        return kind, low, first, ((high - low) * BLOCK, count * BLOCK)
+
+    pieces = range(len(SPLIT))
+    queue = [(kind, unit, part) for unit in pieces for part in range(PARTS) for kind in (0, 1)]
+    queue += [(DOWN, unit, part) for unit in pieces for part in range(PARTS)]
+    queue = [(name, piece_of(*name)) for name in queue]
+    queue = [item for item in queue if item[1][3][0] > 0]
+    everything = 3 * depth * gate_q.shape[1]
+
+    def take(share, needed=()):
+        names, plan, size = [], [], 0
+        while queue:
+            name, piece = queue[0]
+            size += piece[3][0] * piece[3][1]
+            if size * 1000 > share * everything and name[:2] not in needed:
+                break
+            queue.pop(0)
+            names.append(name)
+            plan.append(piece)
+        return names, Fetch(plan)
+
+    def needed_after(step):
+        for op, unit, share in STEPS[step + 1 :]:
+            if op == "up":
+                return ((0, unit), (1, unit))
+            if op in ("down", "last"):
+                return ((DOWN, unit),)
+            if share:
+                return ()
+        return ()
+
+    def held_pieces(kind, unit):
+        return [held[kind, unit, part] for part in range(PARTS) if (kind, unit, part) in held]
 
     rows = [activations] + [swap(activations, "gy", gy, r) for r in range(1, gy)]
-    rows[0], (*scales, down_s), arrays = head(activations, (gate_s, up_s), down_s, weights, planned(HEAD))
-    held = dict(zip(HEAD, arrays))
+    names, fetch = take(HEAD, needed_after(-1))
+    rows[0], (*scales, down_s), arrays = head(activations, (gate_s, up_s), down_s, weights, fetch)
+    held = dict(zip(names, arrays))
 
     sums, hidden, total, after = {}, {}, None, []
-    for op, unit, names in STEPS:
+    for step, (op, unit, share) in enumerate(STEPS):
+        names, fetch = take(share, needed_after(step)) if share else ((), Fetch([]))
         arrays = []
         if op == "up":
             keep, send, ordered, arrays = gate_up(
-                rows, at[unit], pieces("g", unit), pieces("u", unit), scales, weights, planned(names), after
+                rows, at[unit], held_pieces(0, unit), held_pieces(1, unit), scales, weights, fetch, after
             )
             rows = list(ordered) or rows
             sums[unit] = (keep, swap(send, "gx", gx, 1))
             after = [keep]
         elif op == "join":
-            for step in later:
+            for hop in later:
                 keep, send = join(*sums[unit], after)
-                sums[unit] = (keep, swap(send, "gx", gx, step))
+                sums[unit] = (keep, swap(send, "gx", gx, hop))
                 after = [keep]
         elif op == "act":
             own = activate(*sums[unit], after)
             hidden[unit] = (own, swap(own, "gx", gx, 1))
             after = [own]
         elif op == "fetch":
-            arrays = fetch_only(weights, planned(names), after)
+            arrays = fetch_only(weights, fetch, after)
             after = [arrays[0]]
         else:
             outs, arrays = down(
@@ -407,10 +422,10 @@
                 *hidden[unit],
                 total,
                 at[unit],
-                pieces("d", unit),
+                held_pieces(DOWN, unit),
                 down_s,
                 weights,
-                planned(names),
+                fetch,
                 after,
                 op == "last",
             )

time: 73.4 us -> 64.4 us (0.88)
  Pallas kernels: 46.2 us -> 39.6 us
  starting transfers between devices: 18.2 us -> 15.4 us
  waiting for transfers between devices: 6.8 us -> 8.35 us
  local copies, waits for them, and re-layouts: 0.9 us -> 0 us
    pallas_call x26 -> x16, Pallas kernels: 46.2 us -> 39.6 us  [call(): pl.pallas_call(kernel, out_shape=outs, in_specs=specs, out_specs=[IN_VMEM...]
    ppermute x21 -> x15, starting transfers between devices: 18.2 us -> 15.4 us  [swap(): return lax.ppermute(value, axis, [(i, i ^ step) for i in range(size)])]
    ppermute x21 -> x15, waiting for transfers between devices: 6.8 us -> 8.35 us  [swap(): return lax.ppermute(value, axis, [(i, i ^ step) for i in range(size)])]
    unnamed x4 -> x0, local copies, waits for them, and re-layouts: 0.9 us -> none
  transfers between devices with their start and end apart: 21 -> 15, of which waited for: 4 -> 3; matrix products, arithmetic and copies ran while one was open for 0% -> 0% of each run, Pallas kernels for 55% -> 51%
where the time goes in v3:
time: 64.4 us; the launch traced here: 64.2 us
  Pallas kernels  39.6 us (61%)
  starting transfers between devices  15.4 us (24%)
  waiting for transfers between devices  8.35 us (13%)
  other arithmetic  0.67 us (1%)
    pallas_call x16, Pallas kernels, call(): pl.pallas_call(kernel, out_shape=outs, in_specs=specs, out_specs=[IN_VMEM...  39.6 us
    ppermute x15, starting transfers between devices, swap(): return lax.ppermute(value, axis, [(i, i ^ step) for i in range(size)])  15.4 us
    ppermute x15, waiting for transfers between devices, swap(): return lax.ppermute(value, axis, [(i, i ^ step) for i in range(size)])  8.35 us
  transfers between devices with their start and end apart: 15, of which 3 were waited for; matrix products, arithmetic and copies ran while one was open for 0% of the time, Pallas kernels for 51%

profile of v3, /device:TPU:0, one launch (start us, length us, event | category | flops | bytes accessed | tf_op | source)
XLA Modules:
  0.0 64.2 jit_solution(5358133999268697373)
XLA Ops:
  0.0 3.0 %collective-permute-start = (bf16[16,2048]{1,0:T(8,128)(2,1)}, bf16[16,2048]{1,0:T(8,128)(2,1)S(1)}, u32[]{:S(2)}, u32[]{:S(2)}) collective-permute-start(bf16[16,2048]{1,0:T(8,128)(2,1)} %refs_0_.4), channel_id=1, source_target_pairs={{0,1},{1,0},{2,3},{3,2},{4,5},{5,4},{6,7},{7,6},{8,9},{9,8},{10,11... | collective-permute-start | bytes 196616 | tf_op jit(solution)/shard_map/ppermute | solution.py:41
  3.0 2.5 %collective-permute-start.2 = (bf16[16,2048]{1,0:T(8,128)(2,1)}, bf16[16,2048]{1,0:T(8,128)(2,1)S(1)}, u32[]{:S(2)}, u32[]{:S(2)}) collective-permute-start(bf16[16,2048]{1,0:T(8,128)(2,1)} %refs_0_.4), channel_id=1, source_target_pairs={{0,3},{1,2},{2,1},{3,0},{4,7},{5,6},{6,5},{7,4},{8,11},{9,10},{10,... | collective-permute-start | bytes 196616 | tf_op jit(solution)/shard_map/ppermute | solution.py:41
  5.5 0.1 collective-permute-start.1
  5.6 8.8 %shard_map.73 = (bf16[16,2048]{1,0:T(8,128)(2,1)S(1)}, f32[16,7680]{1,0:T(8,128)S(1)}, f32[16,7680]{1,0:T(8,128)S(1)}, f32[60,2048]{1,0:T(8,128)S(1)}, bf16[256,...) custom-call(bf16[16,2048]{1,0:T(8,128)(2,1)} %refs_0_.4, ...), custom_call_target="tpu_custom_call" | custom-call | bytes 25165824 | tf_op jit(solution)/shard_map/pallas_call | solution.py:62
  14.4 0.0 collective-permute-done.refs_1_
  14.4 0.0 collective-permute-done.2.refs_3_
  14.4 0.0 collective-permute-done.1.refs_2_
  14.5 5.3 %shard_map.74 = (f32[64,3072]{1,0:T(8,128)S(1)}, bf16[64,3072]{1,0:T(8,128)(2,1)S(1)}, bf16[64,2048]{1,0:T(8,128)(2,1)S(1)}, bf16[256,2560]{1,0:T(8,128)(2,1)S(1...) custom-call(bf16[16,2048]{1,0:T(8,128)(2,1)S(1)} %get-tuple-element., ...), custom_call_target="tpu_custom_call" | custom-call | flops 1610612736 | bytes 39583744 | tf_op jit(solution)/shard_map/pallas_call | solution.py:62
  19.8 0.1 collective-permute-start.3
  19.9 2.9 %shard_map.75 = (bf16[256,2560]{1,0:T(8,128)(2,1)S(1)}, bf16[256,2560]{1,0:T(8,128)(2,1)S(1)}, bf16[256,2560]{1,0:T(8,128)(2,1)S(1)}, bf16[256,2560]{1,0:T(8,128)(2,1)S(1)}, bf16[256,2560]{1,0:T(8,128)(2,1)S(1)}) custom-call(bf16[2048,7680]{1,0:T(8,128)(2,1)} %refs_12_.5, bf16[2048,7680]{1,0:T(8,128)(2,1)} %refs_13_.5, bf16[7680,2048]{1,0:T(8,128)(2,1)} %refs_14_.3, ...), custom_call_target="tpu_custom_call" | custom-call | bytes 6553600 | tf_op jit(solution)/shard_map/pallas_call | solution.py:62
  22.8 0.0 collective-permute-done.3.got_ref
  22.8 0.1 shard_map.76
  23.0 1.6 %collective-permute-start.4 = (bf16[64,3072]{1,0:T(8,128)(2,1)S(1)}, bf16[64,3072]{1,0:T(8,128)(2,1)S(1)}, u32[]{:S(2)}, u32[]{:S(2)}) collective-permute-start(bf16[64,3072]{1,0:T(8,128)(2,1)S(1)} %get-tuple-element.156), channel_id=1, source_target_pairs={{0,8},{4,12},{8,0},{12,4},{1,9},{5,13},{9,1},{13,5},{2,10},{6,14},... | collective-permute-start | bytes 1179656 | tf_op jit(solution)/shard_map/ppermute | solution.py:41
  24.5 5.0 %shard_map.77 = (f32[64,2560]{1,0:T(8,128)S(1)}, bf16[64,2560]{1,0:T(8,128)(2,1)S(1)}, bf16[256,2048]{1,0:T(8,128)(2,1)S(1)}, bf16[256,2048]{1,0:T(8,128)(2,1)S(...) custom-call(bf16[64,2048]{1,0:T(8,128)(2,1)S(1)} %get-tuple-element., ...), custom_call_target="tpu_custom_call" | custom-call | flops 1342177280 | bytes 34603008 | tf_op jit(solution)/shard_map/pallas_call | solution.py:62
  29.6 0.3 collective-permute-start.5
  29.8 2.4 %shard_map.78 = (bf16[256,2048]{1,0:T(8,128)(2,1)S(1)}, bf16[256,2048]{1,0:T(8,128)(2,1)S(1)}, bf16[256,2048]{1,0:T(8,128)(2,1)S(1)}, bf16[384,2048]{1,0:T(8,128)(2,1)S(1)}) custom-call(bf16[2048,7680]{1,0:T(8,128)(2,1)} %refs_12_.5, bf16[2048,7680]{1,0:T(8,128)(2,1)} %refs_13_.5, bf16[7680,2048]{1,0:T(8,128)(2,1)} %refs_14_.3, ...), custom_call_target="tpu_custom_call" | custom-call | bytes 4718592 | tf_op jit(solution)/shard_map/pallas_call | solution.py:62
  32.2 0.0 collective-permute-done.5.got_ref
  32.3 0.1 shard_map.79
  32.4 0.6 collective-permute-start.8
  33.0 1.6 %collective-permute-done.4.got_ref = bf16[64,3072]{1,0:T(8,128)(2,1)S(1)} collective-permute-done((bf16[64,3072]{1,0:T(8,128)(2,1)S(1)}, bf16[64,3072]{1,0:T(8,128)(2,1)S(1)}, u32[]{:S(2)}, u32[]{:S(2)}) %collective-permute-start.4) | collective-permute-done | bytes 393248 | tf_op jit(solution)/shard_map/ppermute | solution.py:41
  34.5 0.1 shard_map.80.refs_22_.refs_0_
  34.7 3.8 %shard_map.81 = (f32[64,2048]{1,0:T(8,128)S(1)}, bf16[64,2048]{1,0:T(8,128)(2,1)S(1)}, bf16[384,2048]{1,0:T(8,128)(2,1)S(1)}, bf16[384,2048]{1,0:T(8,128)(2,1)S(...) custom-call(bf16[64,2048]{1,0:T(8,128)(2,1)S(1)} %get-tuple-element., ...), custom_call_target="tpu_custom_call" | custom-call | flops 1073741824 | bytes 26214400 | tf_op jit(solution)/shard_map/pallas_call | solution.py:62
  38.5 0.1 collective-permute-start.6
  38.6 0.5 collective-permute-start.10
  39.1 2.5 %shard_map.82 = (bf16[384,2048]{1,0:T(8,128)(2,1)S(1)}, bf16[256,2048]{1,0:T(8,128)(2,1)S(1)}, bf16[384,2048]{1,0:T(8,128)(2,1)S(1)}, bf16[256,2048]{1,0:T(8,128)(2,1)S(1)}) custom-call(bf16[2048,7680]{1,0:T(8,128)(2,1)} %refs_12_.5, bf16[2048,7680]{1,0:T(8,128)(2,1)} %refs_13_.5, bf16[7680,2048]{1,0:T(8,128)(2,1)} %refs_14_.3, ...), custom_call_target="tpu_custom_call" | custom-call | bytes 5242880 | tf_op jit(solution)/shard_map/pallas_call | solution.py:62
  41.6 0.0 collective-permute-done.6.got_ref
  41.6 0.1 shard_map.83
  41.7 1.7 %collective-permute-start.7 = (bf16[64,2048]{1,0:T(8,128)(2,1)S(1)}, bf16[64,2048]{1,0:T(8,128)(2,1)S(1)}, u32[]{:S(2)}, u32[]{:S(2)}) collective-permute-start(bf16[64,2048]{1,0:T(8,128)(2,1)S(1)} %get-tuple-element.163), channel_id=1, source_target_pairs={{0,8},{4,12},{8,0},{12,4},{1,9},{5,13},{9,1},{13,5},{2,10},{6,14},... | collective-permute-start | bytes 786440 | tf_op jit(solution)/shard_map/ppermute | solution.py:41
  43.4 0.0 collective-permute-done.8.got_ref
  43.4 0.1 shard_map.84.refs_14_.refs_0_
  43.5 0.1 collective-permute-start.9
  43.6 0.0 collective-permute-done.10.refs_1_
  43.6 3.0 %shard_map.85 = (f32[64,2048]{1,0:T(8,128)S(1)}, bf16[384,2048]{1,0:T(8,128)(2,1)S(1)}, bf16[256,2048]{1,0:T(8,128)(2,1)S(1)}, bf16[384,2048]{1,0:T(8,128)(2,1)S...) custom-call(bf16[64,1536]{1,0:T(8,128)(2,1)S(1)} %shard_map.80.refs_22_.refs_0_, ...), custom_call_target="tpu_custom_call" | custom-call | flops 805306368 | bytes 19398656 | tf_op jit(solution)/shard_map/pallas_call | solution.py:62
  46.7 0.0 collective-permute-done.9.refs_1_
  46.7 3.5 %shard_map.86 = (f32[64,2048]{1,0:T(8,128)S(1)}, bf16[256,2048]{1,0:T(8,128)(2,1)S(1)}, bf16[256,2048]{1,0:T(8,128)(2,1)S(1)}, bf16[256,2048]{1,0:T(8,128)(2,1)S...) custom-call(bf16[64,1280]{1,0:T(8,128)(2,1)S(1)} %shard_map.84.refs_, ...), custom_call_target="tpu_custom_call" | custom-call | flops 671088640 | bytes 18874368 | tf_op jit(solution)/shard_map/pallas_call | solution.py:62
  50.2 0.0 collective-permute-done.7.got_ref
  50.2 0.1 shard_map.87.refs_0_.refs_15_
  50.3 0.5 collective-permute-start.11
  50.8 1.0 %collective-permute-done.11.refs_1_ = bf16[64,1024]{1,0:T(8,128)(2,1)S(1)} collective-permute-done((bf16[64,1024]{1,0:T(8,128)(2,1)S(1)}, bf16[64,1024]{1,0:T(8,128)(2,1)S(1)}, u32[]{:S(2)}, u32[]{:S(2)}) %collective-permute-start.11) | collective-permute-done | bytes 131104 | tf_op jit(solution)/shard_map/ppermute | solution.py:41
  51.8 1.5 %shard_map.88 = (f32[16,2048]{1,0:T(8,128)S(1)}, bf16[16,2048]{1,0:T(8,128)(2,1)S(1)}, bf16[16,2048]{1,0:T(8,128)(2,1)S(1)}, bf16[16,2048]{1,0:T(8,128)(2,1)S(1)}) custom-call(bf16[64,1024]{1,0:T(8,128)(2,1)S(1)} %shard_map.87.refs_0_.refs_15_, bf16[64,1024]{1,0:T(8,128)(2,1)S(1)} %collective-permute-done.11.refs_1_, ...), custom_call_target="tpu_custom_call" | custom-call | flops 536870912 | bytes 8388608 | tf_op jit(solution)/shard_map/pallas_call | solution.py:62
  53.3 1.9 %collective-permute-start.12 = (bf16[16,2048]{1,0:T(8,128)(2,1)S(1)}, bf16[16,2048]{1,0:T(8,128)(2,1)S(1)}, u32[]{:S(2)}, u32[]{:S(2)}) collective-permute-start(bf16[16,2048]{1,0:T(8,128)(2,1)S(1)} %get-tuple-element.192), channel_id=1, source_target_pairs={{0,1},{1,0},{2,3},{3,2},{4,5},{5,4},{6,7},{7,6},{8,9},{9,8},{10,11... | collective-permute-start | bytes 196616 | tf_op jit(solution)/shard_map/ppermute | solution.py:41
  55.2 1.7 %collective-permute-start.13 = (bf16[16,2048]{1,0:T(8,128)(2,1)S(1)}, bf16[16,2048]{1,0:T(8,128)(2,1)S(1)}, u32[]{:S(2)}, u32[]{:S(2)}) collective-permute-start(bf16[16,2048]{1,0:T(8,128)(2,1)S(1)} %get-tuple-element.193), channel_id=1, source_target_pairs={{0,2},{1,3},{2,0},{3,1},{4,6},{5,7},{6,4},{7,5},{8,10},{9,11},{10,... | collective-permute-start | bytes 196616 | tf_op jit(solution)/shard_map/ppermute | solution.py:41
  56.9 0.9 %collective-permute-start.14 = (bf16[16,2048]{1,0:T(8,128)(2,1)S(1)}, bf16[16,2048]{1,0:T(8,128)(2,1)S(1)}, u32[]{:S(2)}, u32[]{:S(2)}) collective-permute-start(bf16[16,2048]{1,0:T(8,128)(2,1)S(1)} %get-tuple-element.194), channel_id=1, source_target_pairs={{0,3},{1,2},{2,1},{3,0},{4,7},{5,6},{6,5},{7,4},{8,11},{9,10},{10,... | collective-permute-start | bytes 196616 | tf_op jit(solution)/shard_map/ppermute | solution.py:41
  57.8 0.0 collective-permute-done.12
  57.8 5.8 %collective-permute-done.13 = bf16[16,2048]{1,0:T(8,128)(2,1)S(1)} collective-permute-done((bf16[16,2048]{1,0:T(8,128)(2,1)S(1)}, bf16[16,2048]{1,0:T(8,128)(2,1)S(1)}, u32[]{:S(2)}, u32[]{:S(2)}) %collective-permute-start.13) | collective-permute-done | bytes 65568 | tf_op jit(solution)/shard_map/ppermute | solution.py:41
  63.5 0.0 collective-permute-done.14
  63.5 0.7 %add_convert_fusion = bf16[16,2048]{1,0:T(8,128)(2,1)} fusion(bf16[16,2048]{1,0:T(8,128)(2,1)S(1)} %collective-permute-done.14, bf16[16,2048]{1,0:T(8,128)(2,1)S(1)} %collective-permute-done.13, f32[16,2048]{1,0:T(8,128)S(1)} %get-tuple-element.191, bf16[16,2048]{1,0:T(8,128)(2,1)S(1)} %collective-permute-done.12), kind=kLoop, calls=%fused_computation | loop fusion | flops 229376 | bytes 393216 | tf_op jit(solution)/shard_map/convert_element_type | solution.py:437
Async XLA Ops:
  0.0 14.4 %collective-permute-start = (bf16[16,2048]{1,0:T(8,128)(2,1)}, bf16[16,2048]{1,0:T(8,128)(2,1)S(1)}, u32[]{:S(2)}, u32[]{:S(2)}) collective-permute-start(bf16[16,2048]{1,0:T(8,128)(2,1)} %refs_0_.4), channel_id=1, source_target_pairs={{0,1},{1,0},{2,3},{3,2},{4,5},{5,4},{6,7},{7,6},{8,9},{9,8},{10,11... | collective-permute-start | bytes 196616 | tf_op jit(solution)/shard_map/ppermute | solution.py:41
  3.0 11.4 %collective-permute-start.2 = (bf16[16,2048]{1,0:T(8,128)(2,1)}, bf16[16,2048]{1,0:T(8,128)(2,1)S(1)}, u32[]{:S(2)}, u32[]{:S(2)}) collective-permute-start(bf16[16,2048]{1,0:T(8,128)(2,1)} %refs_0_.4), channel_id=1, source_target_pairs={{0,3},{1,2},{2,1},{3,0},{4,7},{5,6},{6,5},{7,4},{8,11},{9,10},{10,... | collective-permute-start | bytes 196616 | tf_op jit(solution)/shard_map/ppermute | solution.py:41
  5.5 8.9 %collective-permute-start.1 = (bf16[16,2048]{1,0:T(8,128)(2,1)}, bf16[16,2048]{1,0:T(8,128)(2,1)S(1)}, u32[]{:S(2)}, u32[]{:S(2)}) collective-permute-start(bf16[16,2048]{1,0:T(8,128)(2,1)} %refs_0_.4), channel_id=1, source_target_pairs={{0,2},{1,3},{2,0},{3,1},{4,6},{5,7},{6,4},{7,5},{8,10},{9,11},{10,... | collective-permute-start | bytes 196616 | tf_op jit(solution)/shard_map/ppermute | solution.py:41
  19.8 3.0 %collective-permute-start.3 = (bf16[64,3072]{1,0:T(8,128)(2,1)S(1)}, bf16[64,3072]{1,0:T(8,128)(2,1)S(1)}, u32[]{:S(2)}, u32[]{:S(2)}) collective-permute-start(bf16[64,3072]{1,0:T(8,128)(2,1)S(1)} %get-tuple-element.137), channel_id=1, source_target_pairs={{0,4},{4,0},{8,12},{12,8},{1,5},{5,1},{9,13},{13,9},{2,6},{6,2},{1... | collective-permute-start | bytes 1179656 | tf_op jit(solution)/shard_map/ppermute | solution.py:41
  23.0 11.6 %collective-permute-start.4 = (bf16[64,3072]{1,0:T(8,128)(2,1)S(1)}, bf16[64,3072]{1,0:T(8,128)(2,1)S(1)}, u32[]{:S(2)}, u32[]{:S(2)}) collective-permute-start(bf16[64,3072]{1,0:T(8,128)(2,1)S(1)} %get-tuple-element.156), channel_id=1, source_target_pairs={{0,8},{4,12},{8,0},{12,4},{1,9},{5,13},{9,1},{13,5},{2,10},{6,14},... | collective-permute-start | bytes 1179656 | tf_op jit(solution)/shard_map/ppermute | solution.py:41
  29.6 2.7 %collective-permute-start.5 = (bf16[64,2560]{1,0:T(8,128)(2,1)S(1)}, bf16[64,2560]{1,0:T(8,128)(2,1)S(1)}, u32[]{:S(2)}, u32[]{:S(2)}) collective-permute-start(bf16[64,2560]{1,0:T(8,128)(2,1)S(1)} %get-tuple-element.157), channel_id=1, source_target_pairs={{0,4},{4,0},{8,12},{12,8},{1,5},{5,1},{9,13},{13,9},{2,6},{6,2},{1... | collective-permute-start | bytes 983048 | tf_op jit(solution)/shard_map/ppermute | solution.py:41
  32.4 11.0 %collective-permute-start.8 = (bf16[64,2560]{1,0:T(8,128)(2,1)S(1)}, bf16[64,2560]{1,0:T(8,128)(2,1)S(1)}, u32[]{:S(2)}, u32[]{:S(2)}) collective-permute-start(bf16[64,2560]{1,0:T(8,128)(2,1)S(1)} %get-tuple-element.164), channel_id=1, source_target_pairs={{0,8},{4,12},{8,0},{12,4},{1,9},{5,13},{9,1},{13,5},{2,10},{6,14},... | collective-permute-start | bytes 983048 | tf_op jit(solution)/shard_map/ppermute | solution.py:41
  38.5 3.1 %collective-permute-start.6 = (bf16[64,2048]{1,0:T(8,128)(2,1)S(1)}, bf16[64,2048]{1,0:T(8,128)(2,1)S(1)}, u32[]{:S(2)}, u32[]{:S(2)}) collective-permute-start(bf16[64,2048]{1,0:T(8,128)(2,1)S(1)} %get-tuple-element.160), channel_id=1, source_target_pairs={{0,4},{4,0},{8,12},{12,8},{1,5},{5,1},{9,13},{13,9},{2,6},{6,2},{1... | collective-permute-start | bytes 786440 | tf_op jit(solution)/shard_map/ppermute | solution.py:41
  38.6 5.0 %collective-permute-start.10 = (bf16[64,1536]{1,0:T(8,128)(2,1)S(1)}, bf16[64,1536]{1,0:T(8,128)(2,1)S(1)}, u32[]{:S(2)}, u32[]{:S(2)}) collective-permute-start(bf16[64,1536]{1,0:T(8,128)(2,1)S(1)} %shard_map.80.refs_22_.refs_0_), channel_id=1, source_target_pairs={{0,4},{4,0},{8,12},{12,8},{1,5},{5,1},{9,13},{13,9},{2,6},{6,2},{1... | collective-permute-start | bytes 589832 | tf_op jit(solution)/shard_map/ppermute | solution.py:41
  41.7 8.4 %collective-permute-start.7 = (bf16[64,2048]{1,0:T(8,128)(2,1)S(1)}, bf16[64,2048]{1,0:T(8,128)(2,1)S(1)}, u32[]{:S(2)}, u32[]{:S(2)}) collective-permute-start(bf16[64,2048]{1,0:T(8,128)(2,1)S(1)} %get-tuple-element.163), channel_id=1, source_target_pairs={{0,8},{4,12},{8,0},{12,4},{1,9},{5,13},{9,1},{13,5},{2,10},{6,14},... | collective-permute-start | bytes 786440 | tf_op jit(solution)/shard_map/ppermute | solution.py:41
  43.5 3.1 %collective-permute-start.9 = (bf16[64,1280]{1,0:T(8,128)(2,1)S(1)}, bf16[64,1280]{1,0:T(8,128)(2,1)S(1)}, u32[]{:S(2)}, u32[]{:S(2)}) collective-permute-start(bf16[64,1280]{1,0:T(8,128)(2,1)S(1)} %shard_map.84.refs_14_.refs_0_), channel_id=1, source_target_pairs={{0,4},{4,0},{8,12},{12,8},{1,5},{5,1},{9,13},{13,9},{2,6},{6,2},{1... | collective-permute-start | bytes 491528 | tf_op jit(solution)/shard_map/ppermute | solution.py:41
  50.3 1.5 %collective-permute-start.11 = (bf16[64,1024]{1,0:T(8,128)(2,1)S(1)}, bf16[64,1024]{1,0:T(8,128)(2,1)S(1)}, u32[]{:S(2)}, u32[]{:S(2)}) collective-permute-start(bf16[64,1024]{1,0:T(8,128)(2,1)S(1)} %shard_map.87.refs_0_.refs_15_), channel_id=1, source_target_pairs={{0,4},{4,0},{8,12},{12,8},{1,5},{5,1},{9,13},{13,9},{2,6},{6,2},{1... | collective-permute-start | bytes 393224 | tf_op jit(solution)/shard_map/ppermute | solution.py:41
  53.3 4.5 %collective-permute-start.12 = (bf16[16,2048]{1,0:T(8,128)(2,1)S(1)}, bf16[16,2048]{1,0:T(8,128)(2,1)S(1)}, u32[]{:S(2)}, u32[]{:S(2)}) collective-permute-start(bf16[16,2048]{1,0:T(8,128)(2,1)S(1)} %get-tuple-element.192), channel_id=1, source_target_pairs={{0,1},{1,0},{2,3},{3,2},{4,5},{5,4},{6,7},{7,6},{8,9},{9,8},{10,11... | collective-permute-start | bytes 196616 | tf_op jit(solution)/shard_map/ppermute | solution.py:41
  55.2 8.4 %collective-permute-start.13 = (bf16[16,2048]{1,0:T(8,128)(2,1)S(1)}, bf16[16,2048]{1,0:T(8,128)(2,1)S(1)}, u32[]{:S(2)}, u32[]{:S(2)}) collective-permute-start(bf16[16,2048]{1,0:T(8,128)(2,1)S(1)} %get-tuple-element.193), channel_id=1, source_target_pairs={{0,2},{1,3},{2,0},{3,1},{4,6},{5,7},{6,4},{7,5},{8,10},{9,11},{10,... | collective-permute-start | bytes 196616 | tf_op jit(solution)/shard_map/ppermute | solution.py:41
  56.9 6.7 %collective-permute-start.14 = (bf16[16,2048]{1,0:T(8,128)(2,1)S(1)}, bf16[16,2048]{1,0:T(8,128)(2,1)S(1)}, u32[]{:S(2)}, u32[]{:S(2)}) collective-permute-start(bf16[16,2048]{1,0:T(8,128)(2,1)S(1)} %get-tuple-element.194), channel_id=1, source_target_pairs={{0,3},{1,2},{2,1},{3,0},{4,7},{5,6},{6,5},{7,4},{8,11},{9,10},{10,... | collective-permute-start | bytes 196616 | tf_op jit(solution)/shard_map/ppermute | solution.py:41

commit v4 on v3

--- a/solution.py
+++ b/solution.py
@@ -8,7 +8,7 @@
 from jax.sharding import PartitionSpec as P
 
 BLOCK = 128
-STRIP = 8
+STRIP = 12
 VMEM_LIMIT = 4 * 2**20
 DOWN = 2
 SPLIT = (24, 20, 16)
@@ -18,17 +18,18 @@
     ("up", 0, 165),
     ("fetch", 0, 60),
     ("join", 0, 0),
-    ("up", 1, 150),
-    ("fetch", 0, 65),
+    ("up", 1, 135),
+    ("fetch", 0, 90),
     ("join", 1, 0),
     ("act", 0, 0),
-    ("up", 2, 100),
-    ("fetch", 0, 60),
+    ("up", 2, 90),
+    ("fetch", 0, 55),
     ("join", 2, 0),
     ("act", 1, 0),
     ("down", 0, 70),
-    ("down", 1, 70),
+    ("down", 1, 60),
     ("act", 2, 0),
+    ("own", 2, 0),
     ("last", 2, 0),
 )
 
@@ -290,7 +291,7 @@
     )[0]
 
 
-def down(gy, own, other, prior, block0, units, scale, weights, fetch, after, last):
+def down(gy, own, other, prior, block0, units, scale, weights, fetch, after, last, only=None):
     total, half = own.shape
     depth, width = sum(u.shape[0] for u in units), units[0].shape[1]
     per = total // gy
@@ -309,12 +310,10 @@
         for copy in copies:
             copy.start()
         core = lax.rem(lax.axis_index("gx"), 2)
-        for slot, ref in enumerate((own_ref, other_ref)):
-            xs[:, pl.ds(pl.multiple_of(lax.rem(core + slot, 2) * half, BLOCK), half)] = ref[...]
-
-        def body(step, carry):
+
+        def body(x, held_w, row0, step, carry):
             columns = pl.ds(pl.multiple_of(step * strip * BLOCK, BLOCK), strip * BLOCK)
-            value = scaled_product(xs, w, scale_ref, block0, columns, columns)
+            value = scaled_product(x, held_w, scale_ref, row0, columns, columns)
             if befores:
                 value = value + befores[0][:, columns]
             if last:
@@ -324,7 +323,24 @@
                 results[0][:, columns] = value
             return carry
 
-        lax.fori_loop(0, width // BLOCK // strip, body, 0)
+        def run(*operands):
+            lax.fori_loop(0, width // BLOCK // strip, functools.partial(body, *operands), 0)
+
+        if only is None:
+            for slot, ref in enumerate((own_ref, other_ref)):
+                xs[:, pl.ds(pl.multiple_of(lax.rem(core + slot, 2) * half, BLOCK), half)] = ref[...]
+            run(xs, w, block0)
+        else:
+            x, parts, rows = (own_ref, other_ref)[only], ([], []), 0
+            for ref in w:
+                parts[rows // half].append(ref)
+                rows += ref.shape[0]
+            for which in (0, 1):
+
+                @pl.when(core == (which + only) % 2)
+                def _():
+                    run(x, parts[which], block0 + which * half // BLOCK)
+
         for copy in copies:
             copy.wait()
 
@@ -368,7 +384,7 @@
         while queue:
             name, piece = queue[0]
             size += piece[3][0] * piece[3][1]
-            if size * 1000 > share * everything and name[:2] not in needed:
+            if names and size * 1000 > share * everything and name[:2] not in needed:
                 break
             queue.pop(0)
             names.append(name)
@@ -379,7 +395,7 @@
         for op, unit, share in STEPS[step + 1 :]:
             if op == "up":
                 return ((0, unit), (1, unit))
-            if op in ("down", "last"):
+            if op in ("down", "own", "last"):
                 return ((DOWN, unit),)
             if share:
                 return ()
@@ -419,7 +435,7 @@
         else:
             outs, arrays = down(
                 gy,
-                *hidden[unit],
+                *((hidden[unit][0],) * 2 if op == "own" else hidden[unit]),
                 total,
                 at[unit],
                 held_pieces(DOWN, unit),
@@ -428,11 +444,12 @@
                 fetch,
                 after,
                 op == "last",
+                {"own": 0, "last": 1}.get(op),
             )
             total = outs[0]
             after = [total]
         held.update(zip(names, arrays))
-    for r in range(1, gy):
+    for r in [*range(2, gy), 1]:
         total = total + swap(outs[r], "gy", gy, r).astype(jnp.float32)
     return total.astype(jnp.bfloat16)
 

time: 64.4 us -> 63 us (0.978)
  waiting for transfers between devices: 8.35 us -> 6.94 us
    ppermute x15, waiting for transfers between devices: 8.35 us -> 6.94 us  [swap(): return lax.ppermute(value, axis, [(i, i ^ step) for i in range(size)])]
    pallas_call x16 -> x17, Pallas kernels: 39.6 us -> 39.9 us  [call(): pl.pallas_call(kernel, out_shape=outs, in_specs=specs, out_specs=[IN_VMEM...]
  transfers between devices with their start and end apart: 15 -> 15, of which waited for: 3 -> 6; matrix products, arithmetic and copies ran while one was open for 0% -> 0% of each run, Pallas kernels for 51% -> 53%
where the time goes in v4:
time: 63 us; the launch traced here: 62.8 us
  Pallas kernels  39.9 us (63%)
  starting transfers between devices  15.1 us (24%)
  waiting for transfers between devices  6.94 us (11%)
  other arithmetic  0.66 us (1%)
    pallas_call x17, Pallas kernels, call(): pl.pallas_call(kernel, out_shape=outs, in_specs=specs, out_specs=[IN_VMEM...  39.9 us
    ppermute x15, starting transfers between devices, swap(): return lax.ppermute(value, axis, [(i, i ^ step) for i in range(size)])  15.1 us
    ppermute x15, waiting for transfers between devices, swap(): return lax.ppermute(value, axis, [(i, i ^ step) for i in range(size)])  6.94 us
  transfers between devices with their start and end apart: 15, of which 6 were waited for; matrix products, arithmetic and copies ran while one was open for 0% of the time, Pallas kernels for 53%

profile of v4, /device:TPU:0, one launch (start us, length us, event | category | flops | bytes accessed | tf_op | source)
XLA Modules:
  0.0 62.8 jit_solution(7220264295084701787)
XLA Ops:
  0.0 3.0 %collective-permute-start = (bf16[16,2048]{1,0:T(8,128)(2,1)}, bf16[16,2048]{1,0:T(8,128)(2,1)S(1)}, u32[]{:S(2)}, u32[]{:S(2)}) collective-permute-start(bf16[16,2048]{1,0:T(8,128)(2,1)} %refs_0_.4), channel_id=1, source_target_pairs={{0,1},{1,0},{2,3},{3,2},{4,5},{5,4},{6,7},{7,6},{8,9},{9,8},{10,11... | collective-permute-start | bytes 196616 | tf_op jit(solution)/shard_map/ppermute | solution.py:42
  3.0 2.5 %collective-permute-start.2 = (bf16[16,2048]{1,0:T(8,128)(2,1)}, bf16[16,2048]{1,0:T(8,128)(2,1)S(1)}, u32[]{:S(2)}, u32[]{:S(2)}) collective-permute-start(bf16[16,2048]{1,0:T(8,128)(2,1)} %refs_0_.4), channel_id=1, source_target_pairs={{0,3},{1,2},{2,1},{3,0},{4,7},{5,6},{6,5},{7,4},{8,11},{9,10},{10,... | collective-permute-start | bytes 196616 | tf_op jit(solution)/shard_map/ppermute | solution.py:42
  5.5 0.1 collective-permute-start.1
  5.6 8.8 %shard_map.73 = (bf16[16,2048]{1,0:T(8,128)(2,1)S(1)}, f32[16,7680]{1,0:T(8,128)S(1)}, f32[16,7680]{1,0:T(8,128)S(1)}, f32[60,2048]{1,0:T(8,128)S(1)}, bf16[256,...) custom-call(bf16[16,2048]{1,0:T(8,128)(2,1)} %refs_0_.4, ...), custom_call_target="tpu_custom_call" | custom-call | bytes 25165824 | tf_op jit(solution)/shard_map/pallas_call | solution.py:63
  14.4 0.0 collective-permute-done.refs_1_
  14.4 0.0 collective-permute-done.2.refs_3_
  14.4 0.0 collective-permute-done.1.refs_2_
  14.5 5.3 %shard_map.74 = (f32[64,3072]{1,0:T(8,128)S(1)}, bf16[64,3072]{1,0:T(8,128)(2,1)S(1)}, bf16[64,2048]{1,0:T(8,128)(2,1)S(1)}, bf16[256,2560]{1,0:T(8,128)(2,1)S(1...) custom-call(bf16[16,2048]{1,0:T(8,128)(2,1)S(1)} %get-tuple-element., ...), custom_call_target="tpu_custom_call" | custom-call | flops 1610612736 | bytes 39583744 | tf_op jit(solution)/shard_map/pallas_call | solution.py:63
  19.8 0.1 collective-permute-start.3
  19.9 2.9 %shard_map.75 = (bf16[256,2560]{1,0:T(8,128)(2,1)S(1)}, bf16[256,2560]{1,0:T(8,128)(2,1)S(1)}, bf16[256,2560]{1,0:T(8,128)(2,1)S(1)}, bf16[256,2560]{1,0:T(8,128)(2,1)S(1)}, bf16[256,2560]{1,0:T(8,128)(2,1)S(1)}) custom-call(bf16[2048,7680]{1,0:T(8,128)(2,1)} %refs_12_.7, bf16[2048,7680]{1,0:T(8,128)(2,1)} %refs_13_.7, bf16[7680,2048]{1,0:T(8,128)(2,1)} %refs_14_.5, ...), custom_call_target="tpu_custom_call" | custom-call | bytes 6553600 | tf_op jit(solution)/shard_map/pallas_call | solution.py:63
  22.8 0.0 collective-permute-done.3.got_ref
  22.8 0.1 shard_map.76
  23.0 1.6 %collective-permute-start.4 = (bf16[64,3072]{1,0:T(8,128)(2,1)S(1)}, bf16[64,3072]{1,0:T(8,128)(2,1)S(1)}, u32[]{:S(2)}, u32[]{:S(2)}) collective-permute-start(bf16[64,3072]{1,0:T(8,128)(2,1)S(1)} %get-tuple-element.156), channel_id=1, source_target_pairs={{0,8},{4,12},{8,0},{12,4},{1,9},{5,13},{9,1},{13,5},{2,10},{6,14},... | collective-permute-start | bytes 1179656 | tf_op jit(solution)/shard_map/ppermute | solution.py:42
  24.5 4.7 %shard_map.77 = (f32[64,2560]{1,0:T(8,128)S(1)}, bf16[64,2560]{1,0:T(8,128)(2,1)S(1)}, bf16[256,2048]{1,0:T(8,128)(2,1)S(1)}, bf16[256,2048]{1,0:T(8,128)(2,1)S(...) custom-call(bf16[64,2048]{1,0:T(8,128)(2,1)S(1)} %get-tuple-element., ...), custom_call_target="tpu_custom_call" | custom-call | flops 1342177280 | bytes 33554432 | tf_op jit(solution)/shard_map/pallas_call | solution.py:63
  29.3 0.3 collective-permute-start.5
  29.5 3.2 %shard_map.78 = (bf16[256,2048]{1,0:T(8,128)(2,1)S(1)}, bf16[256,2048]{1,0:T(8,128)(2,1)S(1)}, bf16[256,2048]{1,0:T(8,128)(2,1)S(1)}, bf16[256,2048]{1,0:T(8,128...) custom-call(bf16[2048,7680]{1,0:T(8,128)(2,1)} %refs_12_.7, bf16[2048,7680]{1,0:T(8,128)(2,1)} %refs_13_.7, ...), custom_call_target="tpu_custom_call" | custom-call | bytes 7340032 | tf_op jit(solution)/shard_map/pallas_call | solution.py:63
  32.8 0.0 collective-permute-done.5.got_ref
  32.8 0.1 shard_map.79
  32.9 0.6 collective-permute-start.8
  33.5 1.1 %collective-permute-done.4.got_ref = bf16[64,3072]{1,0:T(8,128)(2,1)S(1)} collective-permute-done((bf16[64,3072]{1,0:T(8,128)(2,1)S(1)}, bf16[64,3072]{1,0:T(8,128)(2,1)S(1)}, u32[]{:S(2)}, u32[]{:S(2)}) %collective-permute-start.4) | collective-permute-done | bytes 393248 | tf_op jit(solution)/shard_map/ppermute | solution.py:42
  34.6 0.1 shard_map.80.refs_22_.refs_0_
  34.7 3.4 %shard_map.81 = (f32[64,2048]{1,0:T(8,128)S(1)}, bf16[64,2048]{1,0:T(8,128)(2,1)S(1)}, bf16[384,2048]{1,0:T(8,128)(2,1)S(1)}, bf16[384,2048]{1,0:T(8,128)(2,1)S(...) custom-call(bf16[64,2048]{1,0:T(8,128)(2,1)S(1)} %get-tuple-element.119.refs_0_, ...), custom_call_target="tpu_custom_call" | custom-call | flops 1073741824 | bytes 24641536 | tf_op jit(solution)/shard_map/pallas_call | solution.py:63
  38.1 0.1 collective-permute-start.6
  38.1 0.5 collective-permute-start.10
  38.6 2.2 %shard_map.82 = (bf16[384,2048]{1,0:T(8,128)(2,1)S(1)}, bf16[256,2048]{1,0:T(8,128)(2,1)S(1)}, bf16[384,2048]{1,0:T(8,128)(2,1)S(1)}) custom-call(bf16[2048,7680]{1,0:T(8,128)(2,1)} %refs_12_.7, bf16[2048,7680]{1,0:T(8,128)(2,1)} %refs_13_.7, bf16[7680,2048]{1,0:T(8,128)(2,1)} %refs_14_.5, f32[64,2048]{1,0:T(8,128)S(1)} %get-tuple-element.159.refs_3_.keep_ref), custom_call_target="tpu_custom_call" | custom-call | bytes 4194304 | tf_op jit(solution)/shard_map/pallas_call | solution.py:63
  40.9 0.0 collective-permute-done.6.got_ref
  40.9 0.1 shard_map.83
  41.0 1.6 %collective-permute-start.7 = (bf16[64,2048]{1,0:T(8,128)(2,1)S(1)}, bf16[64,2048]{1,0:T(8,128)(2,1)S(1)}, u32[]{:S(2)}, u32[]{:S(2)}) collective-permute-start(bf16[64,2048]{1,0:T(8,128)(2,1)S(1)} %get-tuple-element.163), channel_id=1, source_target_pairs={{0,8},{4,12},{8,0},{12,4},{1,9},{5,13},{9,1},{13,5},{2,10},{6,14},... | collective-permute-start | bytes 786440 | tf_op jit(solution)/shard_map/ppermute | solution.py:42
  42.5 0.3 collective-permute-done.8.got_ref
  42.9 0.1 shard_map.84.refs_14_.refs_0_
  43.0 0.1 collective-permute-start.9
  43.0 0.0 collective-permute-done.10.refs_1_
  43.0 3.4 %shard_map.85 = (f32[64,2048]{1,0:T(8,128)S(1)}, bf16[256,2048]{1,0:T(8,128)(2,1)S(1)}, bf16[384,2048]{1,0:T(8,128)(2,1)S(1)}, bf16[256,2048]{1,0:T(8,128)(2,1)S...) custom-call(bf16[64,1536]{1,0:T(8,128)(2,1)S(1)} %shard_map.80.refs_22_.refs_0_, ...), custom_call_target="tpu_custom_call" | custom-call | flops 805306368 | bytes 20447232 | tf_op jit(solution)/shard_map/pallas_call | solution.py:63
  46.4 0.0 collective-permute-done.9.refs_1_
  46.4 3.5 %shard_map.86 = (f32[64,2048]{1,0:T(8,128)S(1)}, bf16[256,2048]{1,0:T(8,128)(2,1)S(1)}, bf16[256,2048]{1,0:T(8,128)(2,1)S(1)}, bf16[256,2048]{1,0:T(8,128)(2,1)S...) custom-call(bf16[64,1280]{1,0:T(8,128)(2,1)S(1)} %shard_map.84.refs_, ...), custom_call_target="tpu_custom_call" | custom-call | flops 671088640 | bytes 18874368 | tf_op jit(solution)/shard_map/pallas_call | solution.py:63
  49.9 0.0 collective-permute-done.7.got_ref
  49.9 0.1 shard_map.87.refs_0_.refs_1_.refs_15_
  50.0 0.5 collective-permute-start.11
  50.6 0.9 %shard_map.88.refs_2_.refs_15_ = f32[64,2048]{1,0:T(8,128)S(1)} custom-call(bf16[64,1024]{1,0:T(8,128)(2,1)S(1)} %shard_map.87.refs_0_.refs_1_.refs_15_, bf16[64,1024]{1,0:T(8,128)(2,1)S(1)} %shard_map.87.refs_0_.refs_1_.refs_15_, f32[64,2048]{1,0:T(8,128)S(1)} %get-tuple-element.182.rest_0_.refs_2_, bf16[256,2048]{1,0:T(8,128)(2,1)S(1)} %get-tuple-element.183.refs_3_, ...), custom_call_target="tpu_custom_call" | custom-call | flops 536870912 | bytes 8388608 | tf_op jit(solution)/shard_map/pallas_call | solution.py:63
  51.5 0.1 collective-permute-done.11.refs_1_
  51.5 0.9 %shard_map.89 = (f32[16,2048]{1,0:T(8,128)S(1)}, bf16[16,2048]{1,0:T(8,128)(2,1)S(1)}, bf16[16,2048]{1,0:T(8,128)(2,1)S(1)}, bf16[16,2048]{1,0:T(8,128)(2,1)S(1)}) custom-call(bf16[64,1024]{1,0:T(8,128)(2,1)S(1)} %shard_map.87.refs_0_.refs_1_.refs_15_, bf16[64,1024]{1,0:T(8,128)(2,1)S(1)} %collective-permute-done.11.refs_1_, ...), custom_call_target="tpu_custom_call" | custom-call | flops 536870912 | bytes 8388608 | tf_op jit(solution)/shard_map/pallas_call | solution.py:63
  52.5 2.9 %collective-permute-start.12 = (bf16[16,2048]{1,0:T(8,128)(2,1)S(1)}, bf16[16,2048]{1,0:T(8,128)(2,1)S(1)}, u32[]{:S(2)}, u32[]{:S(2)}) collective-permute-start(bf16[16,2048]{1,0:T(8,128)(2,1)S(1)} %get-tuple-element.192), channel_id=1, source_target_pairs={{0,2},{1,3},{2,0},{3,1},{4,6},{5,7},{6,4},{7,5},{8,10},{9,11},{10,... | collective-permute-start | bytes 196616 | tf_op jit(solution)/shard_map/ppermute | solution.py:42
  55.4 1.4 %collective-permute-start.13 = (bf16[16,2048]{1,0:T(8,128)(2,1)S(1)}, bf16[16,2048]{1,0:T(8,128)(2,1)S(1)}, u32[]{:S(2)}, u32[]{:S(2)}) collective-permute-start(bf16[16,2048]{1,0:T(8,128)(2,1)S(1)} %get-tuple-element.193), channel_id=1, source_target_pairs={{0,3},{1,2},{2,1},{3,0},{4,7},{5,6},{6,5},{7,4},{8,11},{9,10},{10,... | collective-permute-start | bytes 196616 | tf_op jit(solution)/shard_map/ppermute | solution.py:42
  56.7 0.0 collective-permute-start.14
  56.7 2.9 %collective-permute-done.12 = bf16[16,2048]{1,0:T(8,128)(2,1)S(1)} collective-permute-done((bf16[16,2048]{1,0:T(8,128)(2,1)S(1)}, bf16[16,2048]{1,0:T(8,128)(2,1)S(1)}, u32[]{:S(2)}, u32[]{:S(2)}) %collective-permute-start.12) | collective-permute-done | bytes 65568 | tf_op jit(solution)/shard_map/ppermute | solution.py:42
  59.6 2.3 %collective-permute-done.13 = bf16[16,2048]{1,0:T(8,128)(2,1)S(1)} collective-permute-done((bf16[16,2048]{1,0:T(8,128)(2,1)S(1)}, bf16[16,2048]{1,0:T(8,128)(2,1)S(1)}, u32[]{:S(2)}, u32[]{:S(2)}) %collective-permute-start.13) | collective-permute-done | bytes 65568 | tf_op jit(solution)/shard_map/ppermute | solution.py:42
  61.9 0.2 collective-permute-done.14
  62.1 0.7 %add_convert_fusion = bf16[16,2048]{1,0:T(8,128)(2,1)} fusion(bf16[16,2048]{1,0:T(8,128)(2,1)S(1)} %collective-permute-done.14, bf16[16,2048]{1,0:T(8,128)(2,1)S(1)} %collective-permute-done.13, f32[16,2048]{1,0:T(8,128)S(1)} %get-tuple-element.191, bf16[16,2048]{1,0:T(8,128)(2,1)S(1)} %collective-permute-done.12), kind=kLoop, calls=%fused_computation | loop fusion | flops 229376 | bytes 393216 | tf_op jit(solution)/shard_map/convert_element_type | solution.py:454
Async XLA Ops:
  0.0 14.4 %collective-permute-start = (bf16[16,2048]{1,0:T(8,128)(2,1)}, bf16[16,2048]{1,0:T(8,128)(2,1)S(1)}, u32[]{:S(2)}, u32[]{:S(2)}) collective-permute-start(bf16[16,2048]{1,0:T(8,128)(2,1)} %refs_0_.4), channel_id=1, source_target_pairs={{0,1},{1,0},{2,3},{3,2},{4,5},{5,4},{6,7},{7,6},{8,9},{9,8},{10,11... | collective-permute-start | bytes 196616 | tf_op jit(solution)/shard_map/ppermute | solution.py:42
  3.0 11.4 %collective-permute-start.2 = (bf16[16,2048]{1,0:T(8,128)(2,1)}, bf16[16,2048]{1,0:T(8,128)(2,1)S(1)}, u32[]{:S(2)}, u32[]{:S(2)}) collective-permute-start(bf16[16,2048]{1,0:T(8,128)(2,1)} %refs_0_.4), channel_id=1, source_target_pairs={{0,3},{1,2},{2,1},{3,0},{4,7},{5,6},{6,5},{7,4},{8,11},{9,10},{10,... | collective-permute-start | bytes 196616 | tf_op jit(solution)/shard_map/ppermute | solution.py:42
  5.5 8.9 %collective-permute-start.1 = (bf16[16,2048]{1,0:T(8,128)(2,1)}, bf16[16,2048]{1,0:T(8,128)(2,1)S(1)}, u32[]{:S(2)}, u32[]{:S(2)}) collective-permute-start(bf16[16,2048]{1,0:T(8,128)(2,1)} %refs_0_.4), channel_id=1, source_target_pairs={{0,2},{1,3},{2,0},{3,1},{4,6},{5,7},{6,4},{7,5},{8,10},{9,11},{10,... | collective-permute-start | bytes 196616 | tf_op jit(solution)/shard_map/ppermute | solution.py:42
  19.8 3.0 %collective-permute-start.3 = (bf16[64,3072]{1,0:T(8,128)(2,1)S(1)}, bf16[64,3072]{1,0:T(8,128)(2,1)S(1)}, u32[]{:S(2)}, u32[]{:S(2)}) collective-permute-start(bf16[64,3072]{1,0:T(8,128)(2,1)S(1)} %get-tuple-element.137), channel_id=1, source_target_pairs={{0,4},{4,0},{8,12},{12,8},{1,5},{5,1},{9,13},{13,9},{2,6},{6,2},{1... | collective-permute-start | bytes 1179656 | tf_op jit(solution)/shard_map/ppermute | solution.py:42
  23.0 11.6 %collective-permute-start.4 = (bf16[64,3072]{1,0:T(8,128)(2,1)S(1)}, bf16[64,3072]{1,0:T(8,128)(2,1)S(1)}, u32[]{:S(2)}, u32[]{:S(2)}) collective-permute-start(bf16[64,3072]{1,0:T(8,128)(2,1)S(1)} %get-tuple-element.156), channel_id=1, source_target_pairs={{0,8},{4,12},{8,0},{12,4},{1,9},{5,13},{9,1},{13,5},{2,10},{6,14},... | collective-permute-start | bytes 1179656 | tf_op jit(solution)/shard_map/ppermute | solution.py:42
  29.3 3.5 %collective-permute-start.5 = (bf16[64,2560]{1,0:T(8,128)(2,1)S(1)}, bf16[64,2560]{1,0:T(8,128)(2,1)S(1)}, u32[]{:S(2)}, u32[]{:S(2)}) collective-permute-start(bf16[64,2560]{1,0:T(8,128)(2,1)S(1)} %get-tuple-element.157), channel_id=1, source_target_pairs={{0,4},{4,0},{8,12},{12,8},{1,5},{5,1},{9,13},{13,9},{2,6},{6,2},{1... | collective-permute-start | bytes 983048 | tf_op jit(solution)/shard_map/ppermute | solution.py:42
  32.9 10.0 %collective-permute-start.8 = (bf16[64,2560]{1,0:T(8,128)(2,1)S(1)}, bf16[64,2560]{1,0:T(8,128)(2,1)S(1)}, u32[]{:S(2)}, u32[]{:S(2)}) collective-permute-start(bf16[64,2560]{1,0:T(8,128)(2,1)S(1)} %get-tuple-element.164), channel_id=1, source_target_pairs={{0,8},{4,12},{8,0},{12,4},{1,9},{5,13},{9,1},{13,5},{2,10},{6,14},... | collective-permute-start | bytes 983048 | tf_op jit(solution)/shard_map/ppermute | solution.py:42
  38.1 2.8 %collective-permute-start.6 = (bf16[64,2048]{1,0:T(8,128)(2,1)S(1)}, bf16[64,2048]{1,0:T(8,128)(2,1)S(1)}, u32[]{:S(2)}, u32[]{:S(2)}) collective-permute-start(bf16[64,2048]{1,0:T(8,128)(2,1)S(1)} %get-tuple-element.160), channel_id=1, source_target_pairs={{0,4},{4,0},{8,12},{12,8},{1,5},{5,1},{9,13},{13,9},{2,6},{6,2},{1... | collective-permute-start | bytes 786440 | tf_op jit(solution)/shard_map/ppermute | solution.py:42
  38.1 4.9 %collective-permute-start.10 = (bf16[64,1536]{1,0:T(8,128)(2,1)S(1)}, bf16[64,1536]{1,0:T(8,128)(2,1)S(1)}, u32[]{:S(2)}, u32[]{:S(2)}) collective-permute-start(bf16[64,1536]{1,0:T(8,128)(2,1)S(1)} %shard_map.80.refs_22_.refs_0_), channel_id=1, source_target_pairs={{0,4},{4,0},{8,12},{12,8},{1,5},{5,1},{9,13},{13,9},{2,6},{6,2},{1... | collective-permute-start | bytes 589832 | tf_op jit(solution)/shard_map/ppermute | solution.py:42
  41.0 9.0 %collective-permute-start.7 = (bf16[64,2048]{1,0:T(8,128)(2,1)S(1)}, bf16[64,2048]{1,0:T(8,128)(2,1)S(1)}, u32[]{:S(2)}, u32[]{:S(2)}) collective-permute-start(bf16[64,2048]{1,0:T(8,128)(2,1)S(1)} %get-tuple-element.163), channel_id=1, source_target_pairs={{0,8},{4,12},{8,0},{12,4},{1,9},{5,13},{9,1},{13,5},{2,10},{6,14},... | collective-permute-start | bytes 786440 | tf_op jit(solution)/shard_map/ppermute | solution.py:42
  43.0 3.5 %collective-permute-start.9 = (bf16[64,1280]{1,0:T(8,128)(2,1)S(1)}, bf16[64,1280]{1,0:T(8,128)(2,1)S(1)}, u32[]{:S(2)}, u32[]{:S(2)}) collective-permute-start(bf16[64,1280]{1,0:T(8,128)(2,1)S(1)} %shard_map.84.refs_14_.refs_0_), channel_id=1, source_target_pairs={{0,4},{4,0},{8,12},{12,8},{1,5},{5,1},{9,13},{13,9},{2,6},{6,2},{1... | collective-permute-start | bytes 491528 | tf_op jit(solution)/shard_map/ppermute | solution.py:42
  50.0 1.5 %collective-permute-start.11 = (bf16[64,1024]{1,0:T(8,128)(2,1)S(1)}, bf16[64,1024]{1,0:T(8,128)(2,1)S(1)}, u32[]{:S(2)}, u32[]{:S(2)}) collective-permute-start(bf16[64,1024]{1,0:T(8,128)(2,1)S(1)} %shard_map.87.refs_0_.refs_1_.refs_15_), channel_id=1, source_target_pairs={{0,4},{4,0},{8,12},{12,8},{1,5},{5,1},{9,13},{13,9},{2,6},{6,2},{1... | collective-permute-start | bytes 393224 | tf_op jit(solution)/shard_map/ppermute | solution.py:42
  52.5 7.1 %collective-permute-start.12 = (bf16[16,2048]{1,0:T(8,128)(2,1)S(1)}, bf16[16,2048]{1,0:T(8,128)(2,1)S(1)}, u32[]{:S(2)}, u32[]{:S(2)}) collective-permute-start(bf16[16,2048]{1,0:T(8,128)(2,1)S(1)} %get-tuple-element.192), channel_id=1, source_target_pairs={{0,2},{1,3},{2,0},{3,1},{4,6},{5,7},{6,4},{7,5},{8,10},{9,11},{10,... | collective-permute-start | bytes 196616 | tf_op jit(solution)/shard_map/ppermute | solution.py:42
  55.4 6.6 %collective-permute-start.13 = (bf16[16,2048]{1,0:T(8,128)(2,1)S(1)}, bf16[16,2048]{1,0:T(8,128)(2,1)S(1)}, u32[]{:S(2)}, u32[]{:S(2)}) collective-permute-start(bf16[16,2048]{1,0:T(8,128)(2,1)S(1)} %get-tuple-element.193), channel_id=1, source_target_pairs={{0,3},{1,2},{2,1},{3,0},{4,7},{5,6},{6,5},{7,4},{8,11},{9,10},{10,... | collective-permute-start | bytes 196616 | tf_op jit(solution)/shard_map/ppermute | solution.py:42
  56.7 5.4 %collective-permute-start.14 = (bf16[16,2048]{1,0:T(8,128)(2,1)S(1)}, bf16[16,2048]{1,0:T(8,128)(2,1)S(1)}, u32[]{:S(2)}, u32[]{:S(2)}) collective-permute-start(bf16[16,2048]{1,0:T(8,128)(2,1)S(1)} %get-tuple-element.194), channel_id=1, source_target_pairs={{0,1},{1,0},{2,3},{3,2},{4,5},{5,4},{6,7},{7,6},{8,9},{9,8},{10,11... | collective-permute-start | bytes 196616 | tf_op jit(solution)/shard_map/ppermute | solution.py:42

commit v5 on v4

--- a/solution.py
+++ b/solution.py
@@ -19,14 +19,14 @@
     ("fetch", 0, 60),
     ("join", 0, 0),
     ("up", 1, 135),
-    ("fetch", 0, 90),
+    ("fetch", 0, 100),
     ("join", 1, 0),
     ("act", 0, 0),
-    ("up", 2, 90),
+    ("up", 2, 95),
     ("fetch", 0, 55),
     ("join", 2, 0),
     ("act", 1, 0),
-    ("down", 0, 70),
+    ("down", 0, 75),
     ("down", 1, 60),
     ("act", 2, 0),
     ("own", 2, 0),

time: 63 us -> 62.6 us (level)
  no operation moved by 1% of the time
where the time goes in v5:
time: 62.6 us; the launch traced here: 62.5 us
  Pallas kernels  39.8 us (64%)
  starting transfers between devices  15.1 us (24%)
  waiting for transfers between devices  6.68 us (11%)
  other arithmetic  0.66 us (1%)
    pallas_call x17, Pallas kernels, call(): pl.pallas_call(kernel, out_shape=outs, in_specs=specs, out_specs=[IN_VMEM...  39.8 us
    ppermute x15, starting transfers between devices, swap(): return lax.ppermute(value, axis, [(i, i ^ step) for i in range(size)])  15.1 us
    ppermute x15, waiting for transfers between devices, swap(): return lax.ppermute(value, axis, [(i, i ^ step) for i in range(size)])  6.68 us
  transfers between devices with their start and end apart: 15, of which 6 were waited for; matrix products, arithmetic and copies ran while one was open for 0% of the time, Pallas kernels for 53%

profile of v5, /device:TPU:0, one launch (start us, length us, event | category | flops | bytes accessed | tf_op | source)
XLA Modules:
  0.0 62.5 jit_solution(8337252596059163988)
XLA Ops:
  0.0 3.0 %collective-permute-start = (bf16[16,2048]{1,0:T(8,128)(2,1)}, bf16[16,2048]{1,0:T(8,128)(2,1)S(1)}, u32[]{:S(2)}, u32[]{:S(2)}) collective-permute-start(bf16[16,2048]{1,0:T(8,128)(2,1)} %refs_0_.4), channel_id=1, source_target_pairs={{0,1},{1,0},{2,3},{3,2},{4,5},{5,4},{6,7},{7,6},{8,9},{9,8},{10,11... | collective-permute-start | bytes 196616 | tf_op jit(solution)/shard_map/ppermute | solution.py:42
  3.0 2.5 %collective-permute-start.2 = (bf16[16,2048]{1,0:T(8,128)(2,1)}, bf16[16,2048]{1,0:T(8,128)(2,1)S(1)}, u32[]{:S(2)}, u32[]{:S(2)}) collective-permute-start(bf16[16,2048]{1,0:T(8,128)(2,1)} %refs_0_.4), channel_id=1, source_target_pairs={{0,3},{1,2},{2,1},{3,0},{4,7},{5,6},{6,5},{7,4},{8,11},{9,10},{10,... | collective-permute-start | bytes 196616 | tf_op jit(solution)/shard_map/ppermute | solution.py:42
  5.5 0.1 collective-permute-start.1
  5.6 8.8 %shard_map.73 = (bf16[16,2048]{1,0:T(8,128)(2,1)S(1)}, f32[16,7680]{1,0:T(8,128)S(1)}, f32[16,7680]{1,0:T(8,128)S(1)}, f32[60,2048]{1,0:T(8,128)S(1)}, bf16[256,...) custom-call(bf16[16,2048]{1,0:T(8,128)(2,1)} %refs_0_.4, ...), custom_call_target="tpu_custom_call" | custom-call | bytes 25165824 | tf_op jit(solution)/shard_map/pallas_call | solution.py:63
  14.4 0.0 collective-permute-done.refs_1_
  14.4 0.0 collective-permute-done.2.refs_3_
  14.4 0.0 collective-permute-done.1.refs_2_
  14.5 5.3 %shard_map.74 = (f32[64,3072]{1,0:T(8,128)S(1)}, bf16[64,3072]{1,0:T(8,128)(2,1)S(1)}, bf16[64,2048]{1,0:T(8,128)(2,1)S(1)}, bf16[256,2560]{1,0:T(8,128)(2,1)S(1...) custom-call(bf16[16,2048]{1,0:T(8,128)(2,1)S(1)} %get-tuple-element., ...), custom_call_target="tpu_custom_call" | custom-call | flops 1610612736 | bytes 39583744 | tf_op jit(solution)/shard_map/pallas_call | solution.py:63
  19.8 0.1 collective-permute-start.3
  19.9 2.9 %shard_map.75 = (bf16[256,2560]{1,0:T(8,128)(2,1)S(1)}, bf16[256,2560]{1,0:T(8,128)(2,1)S(1)}, bf16[256,2560]{1,0:T(8,128)(2,1)S(1)}, bf16[256,2560]{1,0:T(8,128)(2,1)S(1)}, bf16[256,2560]{1,0:T(8,128)(2,1)S(1)}) custom-call(bf16[2048,7680]{1,0:T(8,128)(2,1)} %refs_12_.7, bf16[2048,7680]{1,0:T(8,128)(2,1)} %refs_13_.7, bf16[7680,2048]{1,0:T(8,128)(2,1)} %refs_14_.5, ...), custom_call_target="tpu_custom_call" | custom-call | bytes 6553600 | tf_op jit(solution)/shard_map/pallas_call | solution.py:63
  22.8 0.0 collective-permute-done.3.got_ref
  22.8 0.1 shard_map.76
  23.0 1.6 %collective-permute-start.4 = (bf16[64,3072]{1,0:T(8,128)(2,1)S(1)}, bf16[64,3072]{1,0:T(8,128)(2,1)S(1)}, u32[]{:S(2)}, u32[]{:S(2)}) collective-permute-start(bf16[64,3072]{1,0:T(8,128)(2,1)S(1)} %get-tuple-element.156), channel_id=1, source_target_pairs={{0,8},{4,12},{8,0},{12,4},{1,9},{5,13},{9,1},{13,5},{2,10},{6,14},... | collective-permute-start | bytes 1179656 | tf_op jit(solution)/shard_map/ppermute | solution.py:42
  24.5 4.7 %shard_map.77 = (f32[64,2560]{1,0:T(8,128)S(1)}, bf16[64,2560]{1,0:T(8,128)(2,1)S(1)}, bf16[256,2048]{1,0:T(8,128)(2,1)S(1)}, bf16[256,2048]{1,0:T(8,128)(2,1)S(...) custom-call(bf16[64,2048]{1,0:T(8,128)(2,1)S(1)} %get-tuple-element., ...), custom_call_target="tpu_custom_call" | custom-call | flops 1342177280 | bytes 33554432 | tf_op jit(solution)/shard_map/pallas_call | solution.py:63
  29.3 0.3 collective-permute-start.5
  29.5 3.7 %shard_map.78 = (bf16[256,2048]{1,0:T(8,128)(2,1)S(1)}, bf16[256,2048]{1,0:T(8,128)(2,1)S(1)}, bf16[256,2048]{1,0:T(8,128)(2,1)S(1)}, bf16[256,2048]{1,0:T(8,128...) custom-call(bf16[2048,7680]{1,0:T(8,128)(2,1)} %refs_12_.7, ...), custom_call_target="tpu_custom_call" | custom-call | bytes 8912896 | tf_op jit(solution)/shard_map/pallas_call | solution.py:63
  33.2 0.0 collective-permute-done.5.got_ref
  33.2 0.1 shard_map.79
  33.3 0.6 collective-permute-start.8
  33.9 0.6 %collective-permute-done.4.got_ref = bf16[64,3072]{1,0:T(8,128)(2,1)S(1)} collective-permute-done((bf16[64,3072]{1,0:T(8,128)(2,1)S(1)}, bf16[64,3072]{1,0:T(8,128)(2,1)S(1)}, u32[]{:S(2)}, u32[]{:S(2)}) %collective-permute-start.4) | collective-permute-done | bytes 393248 | tf_op jit(solution)/shard_map/ppermute | solution.py:42
  34.6 0.1 shard_map.80.refs_22_.refs_0_
  34.7 3.6 %shard_map.81 = (f32[64,2048]{1,0:T(8,128)S(1)}, bf16[64,2048]{1,0:T(8,128)(2,1)S(1)}, bf16[384,2048]{1,0:T(8,128)(2,1)S(1)}, bf16[384,2048]{1,0:T(8,128)(2,1)S(...) custom-call(bf16[64,2048]{1,0:T(8,128)(2,1)S(1)} %get-tuple-element., ...), custom_call_target="tpu_custom_call" | custom-call | flops 1073741824 | bytes 25690112 | tf_op jit(solution)/shard_map/pallas_call | solution.py:63
  38.3 0.1 collective-permute-start.6
  38.4 0.5 collective-permute-start.10
  38.9 2.2 %shard_map.82 = (bf16[384,2048]{1,0:T(8,128)(2,1)S(1)}, bf16[256,2048]{1,0:T(8,128)(2,1)S(1)}, bf16[384,2048]{1,0:T(8,128)(2,1)S(1)}) custom-call(bf16[2048,7680]{1,0:T(8,128)(2,1)} %refs_12_.7, bf16[2048,7680]{1,0:T(8,128)(2,1)} %refs_13_.7, bf16[7680,2048]{1,0:T(8,128)(2,1)} %refs_14_.5, f32[64,2048]{1,0:T(8,128)S(1)} %get-tuple-element.159.refs_3_.keep_ref), custom_call_target="tpu_custom_call" | custom-call | bytes 4194304 | tf_op jit(solution)/shard_map/pallas_call | solution.py:63
  41.1 0.0 collective-permute-done.6.got_ref
  41.1 0.1 shard_map.83
  41.2 1.6 %collective-permute-start.7 = (bf16[64,2048]{1,0:T(8,128)(2,1)S(1)}, bf16[64,2048]{1,0:T(8,128)(2,1)S(1)}, u32[]{:S(2)}, u32[]{:S(2)}) collective-permute-start(bf16[64,2048]{1,0:T(8,128)(2,1)S(1)} %get-tuple-element.163), channel_id=1, source_target_pairs={{0,8},{4,12},{8,0},{12,4},{1,9},{5,13},{9,1},{13,5},{2,10},{6,14},... | collective-permute-start | bytes 786440 | tf_op jit(solution)/shard_map/ppermute | solution.py:42
  42.8 0.5 collective-permute-done.8.got_ref
  43.3 0.1 shard_map.84.refs_14_.refs_0_
  43.4 0.1 collective-permute-start.9
  43.5 0.0 collective-permute-done.10.refs_1_
  43.5 2.9 %shard_map.85 = (f32[64,2048]{1,0:T(8,128)S(1)}, bf16[256,2048]{1,0:T(8,128)(2,1)S(1)}, bf16[384,2048]{1,0:T(8,128)(2,1)S(1)}, bf16[256,2048]{1,0:T(8,128)(2,1)S...) custom-call(bf16[64,1536]{1,0:T(8,128)(2,1)S(1)} %shard_map.80.refs_22_.refs_0_, ...), custom_call_target="tpu_custom_call" | custom-call | flops 805306368 | bytes 18874368 | tf_op jit(solution)/shard_map/pallas_call | solution.py:63
  46.4 0.0 collective-permute-done.9.refs_1_
  46.4 3.2 %shard_map.86 = (f32[64,2048]{1,0:T(8,128)S(1)}, bf16[256,2048]{1,0:T(8,128)(2,1)S(1)}, bf16[256,2048]{1,0:T(8,128)(2,1)S(1)}, bf16[256,2048]{1,0:T(8,128)(2,1)S...) custom-call(bf16[64,1280]{1,0:T(8,128)(2,1)S(1)} %shard_map.84.refs_, ...), custom_call_target="tpu_custom_call" | custom-call | flops 671088640 | bytes 17825792 | tf_op jit(solution)/shard_map/pallas_call | solution.py:63
  49.6 0.0 collective-permute-done.7.got_ref
  49.6 0.1 shard_map.87.refs_0_.refs_1_.refs_15_
  49.7 0.5 collective-permute-start.11
  50.2 0.9 %shard_map.88.refs_2_.refs_15_ = f32[64,2048]{1,0:T(8,128)S(1)} custom-call(bf16[64,1024]{1,0:T(8,128)(2,1)S(1)} %shard_map.87.refs_0_.refs_1_.refs_15_, bf16[64,1024]{1,0:T(8,128)(2,1)S(1)} %shard_map.87.refs_0_.refs_1_.refs_15_, f32[64,2048]{1,0:T(8,128)S(1)} %get-tuple-element.182.rest_0_.refs_2_, bf16[256,2048]{1,0:T(8,128)(2,1)S(1)} %get-tuple-element.183.refs_3_, ...), custom_call_target="tpu_custom_call" | custom-call | flops 536870912 | bytes 8388608 | tf_op jit(solution)/shard_map/pallas_call | solution.py:63
  51.1 0.1 collective-permute-done.11.refs_1_
  51.2 0.9 %shard_map.89 = (f32[16,2048]{1,0:T(8,128)S(1)}, bf16[16,2048]{1,0:T(8,128)(2,1)S(1)}, bf16[16,2048]{1,0:T(8,128)(2,1)S(1)}, bf16[16,2048]{1,0:T(8,128)(2,1)S(1)}) custom-call(bf16[64,1024]{1,0:T(8,128)(2,1)S(1)} %shard_map.87.refs_0_.refs_1_.refs_15_, bf16[64,1024]{1,0:T(8,128)(2,1)S(1)} %collective-permute-done.11.refs_1_, ...), custom_call_target="tpu_custom_call" | custom-call | flops 536870912 | bytes 8388608 | tf_op jit(solution)/shard_map/pallas_call | solution.py:63
  52.1 2.9 %collective-permute-start.12 = (bf16[16,2048]{1,0:T(8,128)(2,1)S(1)}, bf16[16,2048]{1,0:T(8,128)(2,1)S(1)}, u32[]{:S(2)}, u32[]{:S(2)}) collective-permute-start(bf16[16,2048]{1,0:T(8,128)(2,1)S(1)} %get-tuple-element.192), channel_id=1, source_target_pairs={{0,2},{1,3},{2,0},{3,1},{4,6},{5,7},{6,4},{7,5},{8,10},{9,11},{10,... | collective-permute-start | bytes 196616 | tf_op jit(solution)/shard_map/ppermute | solution.py:42
  55.0 1.3 %collective-permute-start.13 = (bf16[16,2048]{1,0:T(8,128)(2,1)S(1)}, bf16[16,2048]{1,0:T(8,128)(2,1)S(1)}, u32[]{:S(2)}, u32[]{:S(2)}) collective-permute-start(bf16[16,2048]{1,0:T(8,128)(2,1)S(1)} %get-tuple-element.193), channel_id=1, source_target_pairs={{0,3},{1,2},{2,1},{3,0},{4,7},{5,6},{6,5},{7,4},{8,11},{9,10},{10,... | collective-permute-start | bytes 196616 | tf_op jit(solution)/shard_map/ppermute | solution.py:42
  56.4 0.0 collective-permute-start.14
  56.4 2.9 %collective-permute-done.12 = bf16[16,2048]{1,0:T(8,128)(2,1)S(1)} collective-permute-done((bf16[16,2048]{1,0:T(8,128)(2,1)S(1)}, bf16[16,2048]{1,0:T(8,128)(2,1)S(1)}, u32[]{:S(2)}, u32[]{:S(2)}) %collective-permute-start.12) | collective-permute-done | bytes 65568 | tf_op jit(solution)/shard_map/ppermute | solution.py:42
  59.2 2.4 %collective-permute-done.13 = bf16[16,2048]{1,0:T(8,128)(2,1)S(1)} collective-permute-done((bf16[16,2048]{1,0:T(8,128)(2,1)S(1)}, bf16[16,2048]{1,0:T(8,128)(2,1)S(1)}, u32[]{:S(2)}, u32[]{:S(2)}) %collective-permute-start.13) | collective-permute-done | bytes 65568 | tf_op jit(solution)/shard_map/ppermute | solution.py:42
  61.6 0.2 collective-permute-done.14
  61.8 0.7 %add_convert_fusion = bf16[16,2048]{1,0:T(8,128)(2,1)} fusion(bf16[16,2048]{1,0:T(8,128)(2,1)S(1)} %collective-permute-done.14, bf16[16,2048]{1,0:T(8,128)(2,1)S(1)} %collective-permute-done.13, f32[16,2048]{1,0:T(8,128)S(1)} %get-tuple-element.191, bf16[16,2048]{1,0:T(8,128)(2,1)S(1)} %collective-permute-done.12), kind=kLoop, calls=%fused_computation | loop fusion | flops 229376 | bytes 393216 | tf_op jit(solution)/shard_map/convert_element_type | solution.py:454
Async XLA Ops:
  0.0 14.4 %collective-permute-start = (bf16[16,2048]{1,0:T(8,128)(2,1)}, bf16[16,2048]{1,0:T(8,128)(2,1)S(1)}, u32[]{:S(2)}, u32[]{:S(2)}) collective-permute-start(bf16[16,2048]{1,0:T(8,128)(2,1)} %refs_0_.4), channel_id=1, source_target_pairs={{0,1},{1,0},{2,3},{3,2},{4,5},{5,4},{6,7},{7,6},{8,9},{9,8},{10,11... | collective-permute-start | bytes 196616 | tf_op jit(solution)/shard_map/ppermute | solution.py:42
  3.0 11.4 %collective-permute-start.2 = (bf16[16,2048]{1,0:T(8,128)(2,1)}, bf16[16,2048]{1,0:T(8,128)(2,1)S(1)}, u32[]{:S(2)}, u32[]{:S(2)}) collective-permute-start(bf16[16,2048]{1,0:T(8,128)(2,1)} %refs_0_.4), channel_id=1, source_target_pairs={{0,3},{1,2},{2,1},{3,0},{4,7},{5,6},{6,5},{7,4},{8,11},{9,10},{10,... | collective-permute-start | bytes 196616 | tf_op jit(solution)/shard_map/ppermute | solution.py:42
  5.5 8.9 %collective-permute-start.1 = (bf16[16,2048]{1,0:T(8,128)(2,1)}, bf16[16,2048]{1,0:T(8,128)(2,1)S(1)}, u32[]{:S(2)}, u32[]{:S(2)}) collective-permute-start(bf16[16,2048]{1,0:T(8,128)(2,1)} %refs_0_.4), channel_id=1, source_target_pairs={{0,2},{1,3},{2,0},{3,1},{4,6},{5,7},{6,4},{7,5},{8,10},{9,11},{10,... | collective-permute-start | bytes 196616 | tf_op jit(solution)/shard_map/ppermute | solution.py:42
  19.8 3.0 %collective-permute-start.3 = (bf16[64,3072]{1,0:T(8,128)(2,1)S(1)}, bf16[64,3072]{1,0:T(8,128)(2,1)S(1)}, u32[]{:S(2)}, u32[]{:S(2)}) collective-permute-start(bf16[64,3072]{1,0:T(8,128)(2,1)S(1)} %get-tuple-element.137), channel_id=1, source_target_pairs={{0,4},{4,0},{8,12},{12,8},{1,5},{5,1},{9,13},{13,9},{2,6},{6,2},{1... | collective-permute-start | bytes 1179656 | tf_op jit(solution)/shard_map/ppermute | solution.py:42
  23.0 11.6 %collective-permute-start.4 = (bf16[64,3072]{1,0:T(8,128)(2,1)S(1)}, bf16[64,3072]{1,0:T(8,128)(2,1)S(1)}, u32[]{:S(2)}, u32[]{:S(2)}) collective-permute-start(bf16[64,3072]{1,0:T(8,128)(2,1)S(1)} %get-tuple-element.156), channel_id=1, source_target_pairs={{0,8},{4,12},{8,0},{12,4},{1,9},{5,13},{9,1},{13,5},{2,10},{6,14},... | collective-permute-start | bytes 1179656 | tf_op jit(solution)/shard_map/ppermute | solution.py:42
  29.3 3.9 %collective-permute-start.5 = (bf16[64,2560]{1,0:T(8,128)(2,1)S(1)}, bf16[64,2560]{1,0:T(8,128)(2,1)S(1)}, u32[]{:S(2)}, u32[]{:S(2)}) collective-permute-start(bf16[64,2560]{1,0:T(8,128)(2,1)S(1)} %get-tuple-element.157), channel_id=1, source_target_pairs={{0,4},{4,0},{8,12},{12,8},{1,5},{5,1},{9,13},{13,9},{2,6},{6,2},{1... | collective-permute-start | bytes 983048 | tf_op jit(solution)/shard_map/ppermute | solution.py:42
  33.3 10.0 %collective-permute-start.8 = (bf16[64,2560]{1,0:T(8,128)(2,1)S(1)}, bf16[64,2560]{1,0:T(8,128)(2,1)S(1)}, u32[]{:S(2)}, u32[]{:S(2)}) collective-permute-start(bf16[64,2560]{1,0:T(8,128)(2,1)S(1)} %get-tuple-element.164), channel_id=1, source_target_pairs={{0,8},{4,12},{8,0},{12,4},{1,9},{5,13},{9,1},{13,5},{2,10},{6,14},... | collective-permute-start | bytes 983048 | tf_op jit(solution)/shard_map/ppermute | solution.py:42
  38.3 2.8 %collective-permute-start.6 = (bf16[64,2048]{1,0:T(8,128)(2,1)S(1)}, bf16[64,2048]{1,0:T(8,128)(2,1)S(1)}, u32[]{:S(2)}, u32[]{:S(2)}) collective-permute-start(bf16[64,2048]{1,0:T(8,128)(2,1)S(1)} %get-tuple-element.160), channel_id=1, source_target_pairs={{0,4},{4,0},{8,12},{12,8},{1,5},{5,1},{9,13},{13,9},{2,6},{6,2},{1... | collective-permute-start | bytes 786440 | tf_op jit(solution)/shard_map/ppermute | solution.py:42
  38.4 5.1 %collective-permute-start.10 = (bf16[64,1536]{1,0:T(8,128)(2,1)S(1)}, bf16[64,1536]{1,0:T(8,128)(2,1)S(1)}, u32[]{:S(2)}, u32[]{:S(2)}) collective-permute-start(bf16[64,1536]{1,0:T(8,128)(2,1)S(1)} %shard_map.80.refs_22_.refs_0_), channel_id=1, source_target_pairs={{0,4},{4,0},{8,12},{12,8},{1,5},{5,1},{9,13},{13,9},{2,6},{6,2},{1... | collective-permute-start | bytes 589832 | tf_op jit(solution)/shard_map/ppermute | solution.py:42
  41.2 8.4 %collective-permute-start.7 = (bf16[64,2048]{1,0:T(8,128)(2,1)S(1)}, bf16[64,2048]{1,0:T(8,128)(2,1)S(1)}, u32[]{:S(2)}, u32[]{:S(2)}) collective-permute-start(bf16[64,2048]{1,0:T(8,128)(2,1)S(1)} %get-tuple-element.163), channel_id=1, source_target_pairs={{0,8},{4,12},{8,0},{12,4},{1,9},{5,13},{9,1},{13,5},{2,10},{6,14},... | collective-permute-start | bytes 786440 | tf_op jit(solution)/shard_map/ppermute | solution.py:42
  43.4 3.0 %collective-permute-start.9 = (bf16[64,1280]{1,0:T(8,128)(2,1)S(1)}, bf16[64,1280]{1,0:T(8,128)(2,1)S(1)}, u32[]{:S(2)}, u32[]{:S(2)}) collective-permute-start(bf16[64,1280]{1,0:T(8,128)(2,1)S(1)} %shard_map.84.refs_14_.refs_0_), channel_id=1, source_target_pairs={{0,4},{4,0},{8,12},{12,8},{1,5},{5,1},{9,13},{13,9},{2,6},{6,2},{1... | collective-permute-start | bytes 491528 | tf_op jit(solution)/shard_map/ppermute | solution.py:42
  49.7 1.5 %collective-permute-start.11 = (bf16[64,1024]{1,0:T(8,128)(2,1)S(1)}, bf16[64,1024]{1,0:T(8,128)(2,1)S(1)}, u32[]{:S(2)}, u32[]{:S(2)}) collective-permute-start(bf16[64,1024]{1,0:T(8,128)(2,1)S(1)} %shard_map.87.refs_0_.refs_1_.refs_15_), channel_id=1, source_target_pairs={{0,4},{4,0},{8,12},{12,8},{1,5},{5,1},{9,13},{13,9},{2,6},{6,2},{1... | collective-permute-start | bytes 393224 | tf_op jit(solution)/shard_map/ppermute | solution.py:42
  52.1 7.1 %collective-permute-start.12 = (bf16[16,2048]{1,0:T(8,128)(2,1)S(1)}, bf16[16,2048]{1,0:T(8,128)(2,1)S(1)}, u32[]{:S(2)}, u32[]{:S(2)}) collective-permute-start(bf16[16,2048]{1,0:T(8,128)(2,1)S(1)} %get-tuple-element.192), channel_id=1, source_target_pairs={{0,2},{1,3},{2,0},{3,1},{4,6},{5,7},{6,4},{7,5},{8,10},{9,11},{10,... | collective-permute-start | bytes 196616 | tf_op jit(solution)/shard_map/ppermute | solution.py:42
  55.0 6.6 %collective-permute-start.13 = (bf16[16,2048]{1,0:T(8,128)(2,1)S(1)}, bf16[16,2048]{1,0:T(8,128)(2,1)S(1)}, u32[]{:S(2)}, u32[]{:S(2)}) collective-permute-start(bf16[16,2048]{1,0:T(8,128)(2,1)S(1)} %get-tuple-element.193), channel_id=1, source_target_pairs={{0,3},{1,2},{2,1},{3,0},{4,7},{5,6},{6,5},{7,4},{8,11},{9,10},{10,... | collective-permute-start | bytes 196616 | tf_op jit(solution)/shard_map/ppermute | solution.py:42
  56.4 5.4 %collective-permute-start.14 = (bf16[16,2048]{1,0:T(8,128)(2,1)S(1)}, bf16[16,2048]{1,0:T(8,128)(2,1)S(1)}, u32[]{:S(2)}, u32[]{:S(2)}) collective-permute-start(bf16[16,2048]{1,0:T(8,128)(2,1)S(1)} %get-tuple-element.194), channel_id=1, source_target_pairs={{0,1},{1,0},{2,3},{3,2},{4,5},{5,4},{6,7},{7,6},{8,9},{9,8},{10,11... | collective-permute-start | bytes 196616 | tf_op jit(solution)/shard_map/ppermute | solution.py:42
